TPU v7x, 32 devices: a whole 2x2x4 slice. The times are simulated.
32 devices in a mesh: dp: 8 (over z, y), seq: 4 (over x, core).
Axes of the slice: x: 2, y: 2, z: 4, core: 2. Of those that a mesh axis runs over, the one named last changes fastest.
Arguments:
- frames: bfloat16 [8, 2048, 1024], P('dp', 'seq'), may hold values from -6 to 6
- cotangent: bfloat16 [8, 2048, 1024], P('dp', 'seq'), may hold values from -6 to 6
- lengths: int32 [8, 17], P('dp'), may hold values from 0 to 250, as said below
- attend_weight: bfloat16 [1024, 3072], replicated, may hold values from -0.1875 to 0.1875
- output_weight: bfloat16 [1024, 1024], replicated, may hold values from -0.75 to 0.75
- expand_weight: bfloat16 [1024, 8192], replicated, may hold values from -0.1875 to 0.1875
- shrink_weight: bfloat16 [4096, 1024], replicated, may hold values from -0.09375 to 0.09375
- norm_gains: float32 [2, 1024], replicated, may hold values from 0.25 to 1.75
- norm_biases: float32 [2, 1024], replicated, may hold values from -3 to 3
- layer_scales: float32 [2, 1024], replicated, may hold values from 0.25 to 1.75
Outputs:
- activations: bfloat16 [8, 2048, 1024], P('dp', 'seq')
- input_gradient: bfloat16 [8, 2048, 1024], P('dp', 'seq')
- attend_gradient: float32 [1024, 3072], P('dp')
- output_gradient: float32 [1024, 1024], P('dp')
- expand_gradient: float32 [1024, 8192], P('dp')
- shrink_gradient: float32 [4096, 1024], P(None, 'dp')
- gains_gradient: float32 [2, 1024], P(None, 'dp')
- biases_gradient: float32 [2, 1024], P(None, 'dp')
- scales_gradient: float32 [2, 1024], P(None, 'dp')
Inputs may be any that keep to these rules, and one draw needn't show every extreme that they name: In each stream the first clip has 250 frames and each later one 250 or 125, except the last nonempty clip, which ends at the stream's last frame and may be shorter; the lengths sum to 2048, and the entries after the last nonempty clip are 0.
All inputs are finite; a program needn't handle non-finite values.
Results may differ from a plain program's by a relative error of at most 0.019.
Values may be sent and summed in bfloat16 or wider, within the bound.
No kernel may reach another device: no remote copies, remote signals or barrier semaphores. Data moves between devices by JAX's collectives and lax.ppermute only.
A program may use at most 256 MiB of HBM per device.

v0:
```python
import math

import jax
import jax.numpy as jnp
from jax import lax
from jax.sharding import PartitionSpec as P

D = 1024
HEADS = 16
HEAD_DIM = 64
FF = 4096
WINDOW = 128


def extended_2(block, sides, width):
    for axis, dim in sides:
        count = lax.axis_size(axis)
        forward = [(i, i + 1) for i in range(count - 1)]
        backward = [(target, source) for source, target in forward]
        low = lax.ppermute(
            lax.slice_in_dim(block, block.shape[dim] - width, None, axis=dim), axis, forward
        )
        high = lax.ppermute(lax.slice_in_dim(block, 0, width, axis=dim), axis, backward)
        block = jnp.concatenate([low, block, high], axis=dim)
    return block


def shifted(value, axis, steps):
    count = lax.axis_size(axis)
    initial, last = (max(0, -steps), min(count, count - steps))
    return lax.ppermute(value, axis, [(source, source + steps) for source in range(initial, last)])


def layer_norm_parts(values, gain_row, bias_row):
    row_mean = jnp.mean(values, axis=-1, keepdims=True)
    centered = values - row_mean
    inverse = lax.rsqrt(jnp.mean(centered * centered, axis=-1, keepdims=True) + 1e-05)
    normed = centered * inverse
    return (normed * gain_row + bias_row, normed, inverse)


def layer_norm_back(gradient, normed, inverse, gain_row):
    scaled = gradient * gain_row
    return inverse * (
        scaled
        - jnp.mean(scaled, axis=-1, keepdims=True)
        - normed * jnp.mean(scaled * normed, axis=-1, keepdims=True)
    )


def frame_info(frame_ids, lengths):
    starts = jnp.cumsum(lengths, axis=1) - lengths
    inside = frame_ids[None, :, None] >= starts[:, None, :]
    clip_id = jnp.sum(inside.astype(jnp.int32), axis=2) - 1
    clip_begin = jnp.max(jnp.where(inside, starts[:, None, :], 0), axis=2)
    return (clip_id, clip_begin)


def rotary_tables(positions):
    half_width = HEAD_DIM // 2
    inverse_freq = jnp.exp(
        jnp.arange(half_width, dtype=jnp.float32) * (-2.0 * math.log(10000.0) / HEAD_DIM)
    )
    angles = positions.astype(jnp.float32)[..., None] * inverse_freq
    return (jnp.cos(angles), jnp.sin(angles))


def rotate(values, cosine_table, sine_table):
    half_width = values.shape[-1] // 2
    first_half = values[..., :half_width]
    second_half = values[..., half_width:]
    return jnp.concatenate(
        [
            first_half * cosine_table - second_half * sine_table,
            second_half * cosine_table + first_half * sine_table,
        ],
        axis=-1,
    )


def unrotate(gradient, cosine_table, sine_table):
    half_width = gradient.shape[-1] // 2
    first_half = gradient[..., :half_width]
    second_half = gradient[..., half_width:]
    return jnp.concatenate(
        [
            first_half * cosine_table + second_half * sine_table,
            second_half * cosine_table - first_half * sine_table,
        ],
        axis=-1,
    )


def score_block(queries, keys_rot, allowed):
    scores = jnp.einsum(
        "qhd,khd->hqk", queries, keys_rot, preferred_element_type=jnp.float32
    ) * HEAD_DIM ** (-0.5)
    return jnp.where(allowed[None], scores, -1e30)


def attend(queries, pairs, allowed):
    keys_rot = pairs[:, :D].reshape(-1, HEADS, HEAD_DIM)
    values = pairs[:, D:].reshape(-1, HEADS, HEAD_DIM)
    scores = score_block(queries, keys_rot, allowed)
    row_max = jnp.max(scores, axis=-1, keepdims=True)
    log_total = row_max + jnp.log(jnp.sum(jnp.exp(scores - row_max), axis=-1, keepdims=True))
    weights = jnp.exp(scores - log_total).astype(jnp.bfloat16)
    mixed_heads = jnp.einsum("hqk,khd->qhd", weights, values, preferred_element_type=jnp.float32)
    return (mixed_heads.reshape(queries.shape[0], D), log_total)


def attend_back(queries, pairs, allowed, log_total, grad_mixed):
    keys_rot = pairs[:, :D].reshape(-1, HEADS, HEAD_DIM)
    values = pairs[:, D:].reshape(-1, HEADS, HEAD_DIM)
    weights = jnp.exp(score_block(queries, keys_rot, allowed) - log_total)
    grad_heads = grad_mixed.reshape(-1, HEADS, HEAD_DIM)
    grad_weights = jnp.einsum(
        "qhd,khd->hqk", grad_heads, values, preferred_element_type=jnp.float32
    )
    grad_values = jnp.einsum(
        "hqk,qhd->khd", weights.astype(jnp.bfloat16), grad_heads, preferred_element_type=jnp.float32
    )
    grad_scores = weights * (grad_weights - jnp.sum(weights * grad_weights, axis=-1, keepdims=True))
    grad_scores = grad_scores.astype(jnp.bfloat16)
    grad_queries = jnp.einsum(
        "hqk,khd->qhd", grad_scores, keys_rot, preferred_element_type=jnp.float32
    ) * HEAD_DIM ** (-0.5)
    grad_keys = jnp.einsum(
        "hqk,qhd->khd", grad_scores, queries, preferred_element_type=jnp.float32
    ) * HEAD_DIM ** (-0.5)
    key_rows = pairs.shape[0]
    return (
        grad_queries.reshape(queries.shape[0], D),
        jnp.concatenate(
            [grad_keys.reshape(key_rows, D), grad_values.reshape(key_rows, D)], axis=-1
        ),
    )


def body(
    frames,
    cotangent,
    lengths,
    attend_weight,
    output_weight,
    expand_weight,
    shrink_weight,
    norm_gains,
    norm_biases,
    layer_scales,
):
    stream_count, shard_rows, width = frames.shape
    seq_index = lax.axis_index("seq")
    stream_total = lax.axis_size("seq") * shard_rows
    own_frames = seq_index * shard_rows + jnp.arange(shard_rows, dtype=jnp.int32)
    wide_frames = (
        seq_index * shard_rows - WINDOW + jnp.arange(shard_rows + 2 * WINDOW, dtype=jnp.int32)
    )
    query_clip, query_begin = frame_info(own_frames, lengths)
    key_clip, unused_begin = frame_info(wide_frames, lengths)
    in_stream = (wide_frames >= 0) & (wide_frames < stream_total)
    key_clip = jnp.where(in_stream[None, :], key_clip, -1)
    offset = wide_frames[None, :] - own_frames[:, None]
    allowed = (jnp.abs(offset) <= WINDOW)[None] & (query_clip[:, :, None] == key_clip[:, None, :])
    cosine_table, sine_table = rotary_tables(own_frames[None, :] - query_begin)
    cosine_table = cosine_table[:, :, None, :]
    sine_table = sine_table[:, :, None, :]
    layer_in = frames.astype(jnp.float32)
    normed_one, norm_one, inverse_one = layer_norm_parts(layer_in, norm_gains[0], norm_biases[0])
    normed_one_low = normed_one.astype(jnp.bfloat16)
    projected = jnp.einsum(
        "scd,de->sce", normed_one_low, attend_weight, preferred_element_type=jnp.float32
    )
    head_split = projected.reshape(stream_count, shard_rows, 3, HEADS, HEAD_DIM)
    queries = rotate(head_split[:, :, 0], cosine_table, sine_table).astype(jnp.bfloat16)
    keys_rot = rotate(head_split[:, :, 1], cosine_table, sine_table).reshape(
        stream_count, shard_rows, D
    )
    pairs = jnp.concatenate(
        [keys_rot, head_split[:, :, 2].reshape(stream_count, shard_rows, D)], axis=-1
    ).astype(jnp.bfloat16)
    extended = extended_2(pairs, (("seq", 1),), WINDOW)

    def attend_entry(element):
        return attend(element[0], element[1], element[2])

    mixed_heads, log_total = lax.map(attend_entry, (queries, extended, allowed))
    mixed_low = mixed_heads.astype(jnp.bfloat16)
    attn_branch = jnp.einsum(
        "scd,de->sce", mixed_low, output_weight, preferred_element_type=jnp.float32
    )
    residual = layer_in + attn_branch * layer_scales[0]
    normed_two, norm_two, inverse_two = layer_norm_parts(residual, norm_gains[1], norm_biases[1])
    normed_two_low = normed_two.astype(jnp.bfloat16)
    gate_and_up = jnp.einsum(
        "scd,de->sce", normed_two_low, expand_weight, preferred_element_type=jnp.float32
    )
    gate_part = gate_and_up[..., :FF]
    up_part = gate_and_up[..., FF:]
    sigmoid_gate = jax.nn.sigmoid(gate_part)
    hidden = (gate_part * sigmoid_gate * up_part).astype(jnp.bfloat16)
    mlp_branch = jnp.einsum(
        "scf,fd->scd", hidden, shrink_weight, preferred_element_type=jnp.float32
    )
    activations = (residual + mlp_branch * layer_scales[1]).astype(jnp.bfloat16)
    grad_result = cotangent.astype(jnp.float32)
    scale_grad_two = jnp.sum(grad_result * mlp_branch, axis=(0, 1))
    grad_branch = (grad_result * layer_scales[1]).astype(jnp.bfloat16)
    shrink_grad = jnp.einsum("scf,scd->fd", hidden, grad_branch, preferred_element_type=jnp.float32)
    grad_hidden = jnp.einsum(
        "scd,fd->scf", grad_branch, shrink_weight, preferred_element_type=jnp.float32
    )
    swish_slope = sigmoid_gate * (1.0 + gate_part * (1.0 - sigmoid_gate))
    grad_gate_up = jnp.concatenate(
        [grad_hidden * up_part * swish_slope, grad_hidden * gate_part * sigmoid_gate], axis=-1
    ).astype(jnp.bfloat16)
    expand_grad = jnp.einsum(
        "scd,sce->de", normed_two_low, grad_gate_up, preferred_element_type=jnp.float32
    )
    grad_normed_two = jnp.einsum(
        "sce,de->scd", grad_gate_up, expand_weight, preferred_element_type=jnp.float32
    )
    gain_grad_two = jnp.sum(grad_normed_two * norm_two, axis=(0, 1))
    bias_grad_two = jnp.sum(grad_normed_two, axis=(0, 1))
    grad_residual = grad_result + layer_norm_back(
        grad_normed_two, norm_two, inverse_two, norm_gains[1]
    )
    scale_grad_one = jnp.sum(grad_residual * attn_branch, axis=(0, 1))
    grad_attn = (grad_residual * layer_scales[0]).astype(jnp.bfloat16)
    output_grad = jnp.einsum(
        "scd,sce->de", mixed_low, grad_attn, preferred_element_type=jnp.float32
    )
    grad_mixed = jnp.einsum(
        "sce,de->scd", grad_attn, output_weight, preferred_element_type=jnp.float32
    ).astype(jnp.bfloat16)

    def attend_back_entry(element):
        return attend_back(element[0], element[1], element[2], element[3], element[4])

    grad_queries, grad_pairs = lax.map(
        attend_back_entry, (queries, extended, allowed, log_total, grad_mixed)
    )
    lower_rim = grad_pairs[:, :WINDOW]
    upper_rim = grad_pairs[:, shard_rows + WINDOW :]
    from_lower = shifted(upper_rim.astype(jnp.bfloat16), "seq", 1).astype(upper_rim.dtype)
    from_upper = shifted(lower_rim.astype(jnp.bfloat16), "seq", -1).astype(lower_rim.dtype)
    filler = jnp.zeros((stream_count, shard_rows - WINDOW, 2 * D), jnp.float32)
    own_pairs = (
        grad_pairs[:, WINDOW : WINDOW + shard_rows]
        + jnp.concatenate([from_lower, filler], axis=1)
        + jnp.concatenate([filler, from_upper], axis=1)
    )
    grad_query_rot = unrotate(
        grad_queries.reshape(stream_count, shard_rows, HEADS, HEAD_DIM), cosine_table, sine_table
    ).reshape(stream_count, shard_rows, D)
    grad_key_rot = unrotate(
        own_pairs[..., :D].reshape(stream_count, shard_rows, HEADS, HEAD_DIM),
        cosine_table,
        sine_table,
    ).reshape(stream_count, shard_rows, D)
    grad_projected = jnp.concatenate(
        [grad_query_rot, grad_key_rot, own_pairs[..., D:]], axis=-1
    ).astype(jnp.bfloat16)
    attend_grad = jnp.einsum(
        "scd,sce->de", normed_one_low, grad_projected, preferred_element_type=jnp.float32
    )
    grad_normed_one = jnp.einsum(
        "sce,de->scd", grad_projected, attend_weight, preferred_element_type=jnp.float32
    )
    gain_grad_one = jnp.sum(grad_normed_one * norm_one, axis=(0, 1))
    bias_grad_one = jnp.sum(grad_normed_one, axis=(0, 1))
    input_gradient = (
        grad_residual + layer_norm_back(grad_normed_one, norm_one, inverse_one, norm_gains[0])
    ).astype(jnp.bfloat16)
    gains_grad = jnp.stack([gain_grad_one, gain_grad_two])
    biases_grad = jnp.stack([bias_grad_one, bias_grad_two])
    scales_grad = jnp.stack([scale_grad_one, scale_grad_two])
    summed = (
        lax.psum_scatter(
            attend_grad.astype(jnp.bfloat16), "dp", scatter_dimension=0, tiled=True
        ).astype(jnp.float32),
        lax.psum_scatter(
            output_grad.astype(jnp.bfloat16), "dp", scatter_dimension=0, tiled=True
        ).astype(jnp.float32),
        lax.psum_scatter(
            expand_grad.astype(jnp.bfloat16), "dp", scatter_dimension=0, tiled=True
        ).astype(jnp.float32),
        lax.psum_scatter(
            shrink_grad.astype(jnp.bfloat16), "dp", scatter_dimension=1, tiled=True
        ).astype(jnp.float32),
        lax.psum_scatter(
            gains_grad.astype(jnp.bfloat16), "dp", scatter_dimension=1, tiled=True
        ).astype(jnp.float32),
        lax.psum_scatter(
            biases_grad.astype(jnp.bfloat16), "dp", scatter_dimension=1, tiled=True
        ).astype(jnp.float32),
        lax.psum_scatter(
            scales_grad.astype(jnp.bfloat16), "dp", scatter_dimension=1, tiled=True
        ).astype(jnp.float32),
    )
    summed = (
        lax.psum(summed[0].astype(jnp.bfloat16), "seq").astype(jnp.float32),
        lax.psum(summed[1].astype(jnp.bfloat16), "seq").astype(jnp.float32),
        lax.psum(summed[2].astype(jnp.bfloat16), "seq").astype(jnp.float32),
        lax.psum(summed[3].astype(jnp.bfloat16), "seq").astype(jnp.float32),
        lax.psum(summed[4].astype(jnp.bfloat16), "seq").astype(jnp.float32),
        lax.psum(summed[5].astype(jnp.bfloat16), "seq").astype(jnp.float32),
        lax.psum(summed[6].astype(jnp.bfloat16), "seq").astype(jnp.float32),
    )
    return (
        activations,
        input_gradient,
        summed[0],
        summed[1],
        summed[2],
        summed[3],
        summed[4],
        summed[5],
        summed[6],
    )


def solution(mesh):
    in_specs = (
        P("dp", "seq", None),
        P("dp", "seq", None),
        P("dp", None),
        P(),
        P(),
        P(),
        P(),
        P(),
        P(),
        P(),
    )
    out_specs = (
        P("dp", "seq", None),
        P("dp", "seq", None),
        P("dp", None),
        P("dp", None),
        P("dp", None),
        P(None, "dp"),
        P(None, "dp"),
        P(None, "dp"),
        P(None, "dp"),
    )
    return jax.shard_map(body, mesh=mesh, in_specs=in_specs, out_specs=out_specs, check_vma=False)
```

profile of v0, /device:TPU:0, one launch (start us, length us, event | category | flops | bytes accessed | tf_op | source)
XLA Modules:
  0.0 1072.4 jit_solution(17497278532771493173)
XLA Ops:
  12.7 8.7 copy.26
  49.7 11.0 %fusion = (f32[16,512]{1,0:T(8,128)S(1)}, f32[16,512,768]{2,1,0:T(8,128)}) fusion(pred[512,768]{1,0:T(8,128)(4,1)S(1)} %fusion.35, bf16[768,16,64]{0,2,1:T(8,128)(2,1)S(1)} %bitcast.164, bf16[512,16,32]{0,2,1:T(8,128)(2,1)S(1)} %copy-done.17, bf16[512,16,32]{0,2,1:T(8,128)(2,1)S(1)} %copy-done.15), kind=kOutput, calls=%fused_computation.5 | convolution fusion | flops 826269696 | bytes 28213248 | tf_op jit(solution)/shard_map/while/body/eval_jaxpr/qhd,khd->hqk/dot_general | solution.py:95
  60.7 13.4 %exponential_reduce_fusion = f32[16,512]{1,0:T(8,128)S(1)} fusion(f32[16,512,768]{2,1,0:T(8,128)} %get-tuple-element.108, f32[16,512]{1,0:T(8,128)S(1)} %get-tuple-element.107, pred[512,768]{1,0:T(8,128)(4,1)S(1)} %fusion.35), kind=kLoop, calls=%fused_computation.3 | loop fusion | flops 25157632 | bytes 25624576 | tf_op jit(solution)/shard_map/while/body/eval_jaxpr/reduce_sum | solution.py:106
  74.1 11.3 %convolution_convert_fusion.4 = bf16[16,64,512]{2,1,0:T(8,128)(2,1)S(1)} fusion(bf16[768,16,64]{0,2,1:T(8,128)(2,1)S(1)} %bitcast.173, f32[16,512,768]{2,1,0:T(8,128)} %get-tuple-element.108, f32[16,512]{1,0:T(8,128)S(1)} %log_add_fusion, pred[512,768]{1,0:T(8,128)(4,1)S(1)} %fusion.35), kind=kOutput, calls=%fused_computation.80 | convolution fusion | flops 830996480 | bytes 28213248 | tf_op jit(solution)/shard_map/while/body/eval_jaxpr/hqk,khd->qhd/dot_general | solution.py:108
  88.5 16.4 %convolution_bitcast_fusion = f32[1,512,8192]{2,1,0:T(8,128)} fusion(bf16[1024,8192]{1,0:T(8,128)(2,1)} %param.15, f32[1,512,1024]{2,1,0:T(8,128)S(1)} %get-tuple-element.71, f32[1024]{0:T(1024)S(1)} %bitcast.204, f32[1024]{0:T(1024)S(1)} %bitcast.199, f32[512]{0:T(512)S(1)} %add_rsqrt_fusion, f32[512]{0:T(512)S(1)} %broadcast_multiply_fusion.4), kind=kOutput, calls=%fused_computation.8 | convolution fusion | flops 8592556032 | bytes 35663872 | tf_op jit(solution)/shard_map/scd,de->sce/dot_general | solution.py:195
  104.9 16.8 %fusion.12 = (bf16[512,4096]{1,0:T(8,128)(2,1)}, bf16[512,4096]{1,0:T(8,128)(2,1)}, bf16[1,512,4096]{2,1,0:T(8,128)(2,1)}) fusion(f32[1,512,8192]{2,1,0:T(8,128)} %convolution_bitcast_fusion, bf16[4096,1024]{1,0:T(8,128)(2,1)} %param.16, bf16[1,512,1024]{2,1,0:T(8,128)(2,1)} %param.11, f32[1024]{0:T(1024)S(1)} %bitcast.208), kind=kOutput, calls=%fused_computation.28 | convolution fusion | flops 4330094592 | bytes 38801408 | tf_op jit(solution)/shard_map/scd,fd->scf/dot_general | solution.py:210
  121.8 10.3 convolution_convert_fusion.1
  132.1 11.8 %copy.29 = bf16[4096,1024]{0,1:T(8,128)(2,1)} copy(bf16[4096,1024]{1,0:T(8,128)(2,1)} %convolution_convert_fusion.1) | data formatting | bytes 16777216
  143.9 17.3 %fusion.31 = (bf16[1024]{0:T(1024)(128)(2,1)}, f32[512]{0:T(512)S(1)}, f32[512,1024]{1,0:T(8,128)}) fusion(f32[1,512,1024]{2,1,0:T(8,128)} %copy-done.12, f32[512]{0:T(512)S(1)} %add_rsqrt_fusion, f32[512]{0:T(512)S(1)} %broadcast_multiply_fusion.4, f32[1024]{0:T(1024)S(1)} %bitcast.200, bf16[1024,8192]{1,0:T(8,128)(2,1)} %param.15, ...), kind=kOutput, calls=%fused_computation.62 | convolution fusion | flops 8610379776 | bytes 29372416 | tf_op jit(solution)/shard_map/sce,de->scd/dot_general | solution.py:220
  163.1 13.4 %fusion.29 = (bf16[1024]{0:T(1024)(128)(2,1)}, bf16[1,512,1024]{2,1,0:T(8,128)(2,1)}, bf16[1024]{0:T(1024)(128)(2,1)}, f32[1,512,1024]{2,1,0:T(8,128)S(1)}) fusion(bf16[1,512,1024]{2,1,0:T(8,128)(2,1)} %param.11, f32[1,512,1024]{2,1,0:T(8,128)} %copy-done.12, f32[1024]{0:T(1024)S(1)} %bitcast.210, f32[512,1024]{1,0:T(8,128)} %get-tuple-element.109, ...), kind=kOutput, calls=%fused_computation.54 | convolution fusion | flops 4303353856 | bytes 23089152 | tf_op jit(solution)/shard_map/scf,fd->scd/dot_general | solution.py:202
  186.3 20.0 %multiply_reduce_fusion = (f32[16,512]{1,0:T(8,128)S(1)}, f32[16,512,768]{2,1,0:T(8,128)}) fusion(f32[16,512,768]{2,1,0:T(8,128)} %get-tuple-element.108, f32[16,512]{1,0:T(8,128)S(1)} %copy-done.29, pred[512,768]{1,0:T(8,128)(4,1)S(1)} %fusion.35, bf16[512,16,64]{0,2,1:T(8,128)(2,1)S(1)} %bitcast.176, bf16[768,16,64]{0,2,1:T(8,128)(2,1)S(1)} %bitcast.174), kind=kOutput, calls=%fused_computation.1 | convolution fusion | flops 836755456 | bytes 53411840 | tf_op jit(solution)/shard_map/while/body/eval_jaxpr/qhd,khd->hqk/dot_general | solution.py:117
  206.2 17.5 %multiply_convert_fusion = bf16[16,512,768]{2,1,0:T(8,128)(2,1)S(1)} fusion(f32[16,512,768]{2,1,0:T(8,128)} %get-tuple-element.112, f32[16,512,768]{2,1,0:T(8,128)} %get-tuple-element.108, f32[16,512]{1,0:T(8,128)S(1)} %get-tuple-element.111, f32[16,512]{1,0:T(8,128)S(1)} %copy-done.29, pred[512,768]{1,0:T(8,128)(4,1)S(1)} %fusion.35), kind=kLoop, calls=%fused_computation | loop fusion | flops 37748736 | bytes 63373312 | tf_op jit(solution)/shard_map/while/body/eval_jaxpr/convert_element_type | solution.py:124
  232.2 13.6 %fusion.51 = f32[16,64,768]{2,1,0:T(8,128)} fusion(bf16[512,16,64]{0,2,1:T(8,128)(2,1)S(1)} %bitcast.177, f32[16,512,768]{2,1,0:T(8,128)} %get-tuple-element.108, f32[16,512]{1,0:T(8,128)S(1)} %copy-done.29, pred[512,768]{1,0:T(8,128)(4,1)S(1)} %fusion.35), kind=kOutput, calls=%fused_computation.110 | convolution fusion | flops 830472192 | bytes 29786112 | tf_op jit(solution)/shard_map/while/body/eval_jaxpr/hqk,qhd->khd/dot_general | solution.py:120
  249.2 8.9 collective-permute-start.2
  259.7 9.4 multiply_bitcast_fusion
  273.1 9.2 convolution_convert_fusion.2
  283.0 16.5 %convolution_convert_fusion = bf16[1024,8192]{1,0:T(8,128)(2,1)} fusion(bf16[512,4096]{1,0:T(8,128)(2,1)} %get-tuple-element.73, bf16[512,4096]{1,0:T(8,128)(2,1)} %get-tuple-element.72, f32[1,512,1024]{2,1,0:T(8,128)} %copy-done.12, f32[1024]{0:T(1024)S(1)} %bitcast.205, f32[1024]{0:T(1024)S(1)} %bitcast.203, f32[512]{0:T(512)S(1)} %copy-done.46, ...), kind=kOutput, calls=%fused_computation.6 | convolution fusion | flops 8617721856 | bytes 27275264 | tf_op jit(solution)/shard_map/scd,sce->de/dot_general | solution.py:217
  314.5 56.3 %reduce-scatter.18.cloned.1.call-done = bf16[128,1024]{1,0:T(8,128)(2,1)} async-done(((bf16[1024,1024]{1,0:T(8,128)(2,1)}), bf16[128,1024]{1,0:T(8,128)(2,1)}) %reduce-scatter.18.cloned.1.call-update) | async-done | bytes 262160 | tf_op jit(solution)/shard_map/reduce_scatter | solution.py:282
  370.8 121.0 %reduce-scatter.16.cloned.1.call-done = bf16[128,3072]{1,0:T(8,128)(2,1)} async-done(((bf16[1024,3072]{1,0:T(8,128)(2,1)}), bf16[128,3072]{1,0:T(8,128)(2,1)}) %reduce-scatter.16.cloned.1.call-update) | async-done | bytes 786448 | tf_op jit(solution)/shard_map/reduce_scatter | solution.py:279
  491.8 286.0 %reduce-scatter.20.cloned.1.call-done = bf16[128,8192]{1,0:T(8,128)(2,1)} async-done(((bf16[1024,8192]{1,0:T(8,128)(2,1)}), bf16[128,8192]{1,0:T(8,128)(2,1)}) %reduce-scatter.20.cloned.1.call-update) | async-done | bytes 2097168 | tf_op jit(solution)/shard_map/reduce_scatter | solution.py:285
  777.8 63.4 %reduce-scatter.28.cloned.1.call-done = bf16[128,2]{1,0:T(8,128)(2,1)} async-done(((bf16[1024,2]{1,0:T(8,128)(2,1)}), bf16[128,2]{1,0:T(8,128)(2,1)}) %reduce-scatter.28.cloned.1.call-update) | async-done | bytes 528
  846.0 58.7 %reduce-scatter.26.cloned.1.call-done = bf16[128,2]{1,0:T(8,128)(2,1)} async-done(((bf16[1024,2]{1,0:T(8,128)(2,1)}), bf16[128,2]{1,0:T(8,128)(2,1)}) %reduce-scatter.26.cloned.1.call-update) | async-done | bytes 528
  905.5 63.3 %reduce-scatter.24.cloned.1.call-done = bf16[128,2]{1,0:T(8,128)(2,1)} async-done(((bf16[1024,2]{1,0:T(8,128)(2,1)}), bf16[128,2]{1,0:T(8,128)(2,1)}) %reduce-scatter.24.cloned.1.call-update) | async-done | bytes 528
  977.0 80.1 %all-reduce.6.cloned.1.call-done = (bf16[128,3072]{1,0:T(8,128)(2,1)}, bf16[128,1024]{1,0:T(8,128)(2,1)}, bf16[128,8192]{1,0:T(8,128)(2,1)}, bf16[4096,128]{1,0:T(8,128)(2,1)}) async-done(((bf16[128,3072]{1,0:T(8,128)(2,1)}, bf16[128,1024]{1,0:T(8,128)(2,1)}, bf16[128,8192]{1,0:T(8,128)(2,1)}, bf16[4096,128]{1,0:T(8,128)(2,1)}), (bf16[128,3072]{1,0:T(8,128)(2,1)}, bf16[128,1024]{1,0:T(8,128)(2,1)}, ...) | async-done | bytes 4194320 | tf_op jit(solution)/shard_map/psum | solution.py:302
  (196 shorter events, 103.0 us)
Async XLA Ops:
  7.2 78.3 %copy-start = (bf16[1024,1024]{1,0:T(8,128)(2,1)S(1)}, bf16[1024,1024]{1,0:T(8,128)(2,1)}, u32[]{:S(2)}) copy-start(bf16[1024,1024]{1,0:T(8,128)(2,1)} %param.14) | copy-start | bytes 6291460
  7.2 305.0 %reduce-scatter.22.cloned.1.call-start = ((), (), s32[]{:S(2)}) async-start(), calls=%async_computation.10 | async-start | bytes 9437184
  8.8 12.5 %copy-start.32 = (f32[512]{0:T(512)}, f32[512]{0:T(512)S(1)}, u32[]{:S(2)}) copy-start(f32[512]{0:T(512)S(1)} %broadcast_multiply_fusion.5) | copy-start | bytes 6148
  37.6 5.8 collective-permute-start
  40.7 5.5 collective-permute-start.1
  48.6 12.1 %copy-start.6 = (bf16[768,1024]{0,1:T(8,128)(2,1)}, bf16[768,1024]{0,1:T(8,128)(2,1)S(1)}, u32[]{:S(2)}) copy-start(bf16[768,1024]{0,1:T(8,128)(2,1)S(1)} %get-tuple-element.79) | copy-start | bytes 4718596
  48.6 25.5 %copy-start.13 = (bf16[768,1024]{0,1:T(8,128)(2,1)}, bf16[768,1024]{0,1:T(8,128)(2,1)S(1)}, u32[]{:S(2)}) copy-start(bf16[768,1024]{0,1:T(8,128)(2,1)S(1)} %get-tuple-element.80) | copy-start | bytes 4718596
  74.1 11.4 %copy-start.28 = (f32[16,512]{1,0:T(8,128)}, f32[16,512]{1,0:T(8,128)S(1)}, u32[]{:S(2)}) copy-start(f32[16,512]{1,0:T(8,128)S(1)} %log_add_fusion) | copy-start | bytes 98308
  88.1 16.8 %copy-start.12 = (f32[1,512,1024]{2,1,0:T(8,128)}, f32[1,512,1024]{2,1,0:T(8,128)S(1)}, u32[]{:S(2)}) copy-start(f32[1,512,1024]{2,1,0:T(8,128)S(1)} %get-tuple-element.71) | copy-start | bytes 6291460
  88.5 74.6 %copy-start.45 = (f32[512]{0:T(512)}, f32[512]{0:T(512)S(1)}, u32[]{:S(2)}) copy-start(f32[512]{0:T(512)S(1)} %add_rsqrt_fusion) | copy-start | bytes 6148
  88.5 16.4 %copy-start.41 = (f32[1,1024]{1,0:T(1,128)S(1)}, f32[1,1024]{1,0:T(1,128)}, u32[]{:S(2)}) copy-start(f32[1,1024]{1,0:T(1,128)} %get-tuple-element.99) | copy-start | bytes 12292
  143.9 226.9 %reduce-scatter.18.cloned.1.call-start = ((), (), s32[]{:S(2)}) async-start(), calls=%async_computation.8 | async-start | bytes 2359296 | tf_op jit(solution)/shard_map/reduce_scatter | solution.py:282
  206.2 22.1 %copy-start.16 = (bf16[512,16,32]{0,2,1:T(8,128)(2,1)S(1)}, bf16[512,16,32]{0,2,1:T(8,128)(2,1)}, u32[]{:S(2)}) copy-start(bf16[512,16,32]{0,2,1:T(8,128)(2,1)} %get-tuple-element.85) | copy-start | bytes 1572868
  206.2 22.1 %copy-start.18 = (bf16[512,16,32]{0,2,1:T(8,128)(2,1)S(1)}, bf16[512,16,32]{0,2,1:T(8,128)(2,1)}, u32[]{:S(2)}) copy-start(bf16[512,16,32]{0,2,1:T(8,128)(2,1)} %get-tuple-element.86) | copy-start | bytes 1572868
  245.9 245.9 %reduce-scatter.16.cloned.1.call-start = ((), (), s32[]{:S(2)}) async-start(), calls=%async_computation.7 | async-start | bytes 7077888 | tf_op jit(solution)/shard_map/reduce_scatter | solution.py:279
  249.2 20.4 %collective-permute-start.2 = (bf16[1,128,2048]{1,2,0:T(8,128)(2,1)S(1)}, bf16[1,128,2048]{1,2,0:T(8,128)(2,1)S(1)}, u32[]{:S(2)}, u32[]{:S(2)}) collective-permute-start(bf16[1,128,2048]{1,2,0:T(8,128)(2,1)S(1)} %get-tuple-element.77), channel_id=1, source_target_pairs={{0,1},{1,2},{2,3},{4,5},{5,6},{6,7},{8,9},{9,10},{10,11},{12,13},{... | collective-permute-start | bytes 1572872 | tf_op jit(solution)/shard_map/ppermute | solution.py:31
  258.1 11.0 %copy-start.3 = (f32[16,64,768]{2,1,0:T(8,128)S(1)}, f32[16,64,768]{2,1,0:T(8,128)}, u32[]{:S(2)}) copy-start(f32[16,64,768]{2,1,0:T(8,128)} %convolution_multiply_fusion) | copy-start | bytes 9437188
  258.1 11.0 %copy-start.8 = (f32[16,64,768]{2,1,0:T(8,128)S(1)}, f32[16,64,768]{2,1,0:T(8,128)}, u32[]{:S(2)}) copy-start(f32[16,64,768]{2,1,0:T(8,128)} %fusion.51) | copy-start | bytes 9437188
  258.2 11.5 %collective-permute-start.3 = (bf16[1,128,2048]{1,2,0:T(8,128)(2,1)S(1)}, bf16[1,128,2048]{1,2,0:T(8,128)(2,1)S(1)}, u32[]{:S(2)}, u32[]{:S(2)}) collective-permute-start(bf16[1,128,2048]{1,2,0:T(8,128)(2,1)S(1)} %get-tuple-element.78), channel_id=1, source_target_pairs={{1,0},{2,1},{3,2},{5,4},{6,5},{7,6},{9,8},{10,9},{11,10},{13,12},{... | collective-permute-start | bytes 1572872 | tf_op jit(solution)/shard_map/ppermute | solution.py:31
  282.4 495.4 %reduce-scatter.20.cloned.1.call-start = ((), (), s32[]{:S(2)}) async-start(), calls=%async_computation.9 | async-start | bytes 18874368 | tf_op jit(solution)/shard_map/reduce_scatter | solution.py:285
  299.6 541.7 %reduce-scatter.28.cloned.1.call-start = ((), (), s32[]{:S(2)}) async-start(), calls=%async_computation.13 | async-start | bytes 294912
  301.2 603.5 %reduce-scatter.26.cloned.1.call-start = ((), (), s32[]{:S(2)}) async-start(), calls=%async_computation.12 | async-start | bytes 294912
  311.2 657.7 %reduce-scatter.24.cloned.1.call-start = ((), (), s32[]{:S(2)}) async-start(), calls=%async_computation.11 | async-start | bytes 294912
  312.1 744.9 %all-reduce.6.cloned.1.call-start = ((), (), s32[]{:S(2)}) async-start(), calls=%async_computation.14 | async-start | bytes 8388608 | tf_op jit(solution)/shard_map/psum | solution.py:302
  (36 other events, 121.2 us)
Sparse Core Ops, SparseCore 0:
  144.0 156.1 reduce-scatter.21
  304.1 66.6 reduce-scatter.17
  374.8 116.9 reduce-scatter.15
  495.9 281.8 reduce-scatter.19
  781.0 60.2 reduce-scatter.27
  844.4 60.2 reduce-scatter.25
  908.6 60.1 reduce-scatter.23
  972.0 85.0 all-reduce.5
where the time goes:
time: 1080 us; the launch traced here: 1070 us
  waiting for transfers between devices  732 us (68%)
  matrix products  192 us (18%)
  other arithmetic  64.2 us (6%)
  local copies, waits for them, and re-layouts  48.1 us (4%)
  starting transfers between devices  15.4 us (1%)
  between operations  15.1 us (1%)
    reduce_scatter x1, waiting for transfers between devices, body(): lax.psum_scatter(expand_grad.astype(jnp.bfloat16), 'dp', scatter_dimensio...  286 us
    unnamed x12, waiting for transfers between devices  186 us
    reduce_scatter x1, waiting for transfers between devices, body(): lax.psum_scatter(attend_grad.astype(jnp.bfloat16), 'dp', scatter_dimensio...  121 us
    psum x1, waiting for transfers between devices, body(): lax.psum(summed[0].astype(jnp.bfloat16), 'seq').astype(jnp.float32)  80.1 us
    reduce_scatter x1, waiting for transfers between devices, body(): lax.psum_scatter(output_grad.astype(jnp.bfloat16), 'dp', scatter_dimensio...  56.3 us
    unnamed x105, local copies, waits for them, and re-layouts  39.4 us
  transfers between devices with their start and end apart: 12, of which 8 were waited for; matrix products, arithmetic and copies ran while one was open for 15% of the time, Pallas kernels for 0%

commit v1 on v0

v1 whole, which is shorter than its diff:
```python
import functools
import math

import jax
import jax.numpy as jnp
from jax import lax
from jax.experimental import pallas as pl
from jax.experimental.pallas import tpu as pltpu
from jax.sharding import PartitionSpec as P

D = 1024
HEADS = 16
HEAD_DIM = 64
FF = 4096
WINDOW = 128
QUAD = 4 * HEAD_DIM
SLICES = 8
PART = FF // SLICES
HALF = PART // 2
EPS = 1e-05
BF = jnp.bfloat16
F32 = jnp.float32
VMEM_BYTES = 58 * 1024 * 1024


def dot_nn(a, b):
    return lax.dot_general(a, b, (((1,), (0,)), ((), ())), preferred_element_type=F32)


def dot_nt(a, b):
    return lax.dot_general(a, b, (((1,), (1,)), ((), ())), preferred_element_type=F32)


def dot_tn(a, b):
    return lax.dot_general(a, b, (((0,), (0,)), ((), ())), preferred_element_type=F32)


def params(**extra):
    return pltpu.CompilerParams(vmem_limit_bytes=VMEM_BYTES, **extra)


def cost(flops, size, transcendentals=0):
    return pl.CostEstimate(
        flops=int(flops), bytes_accessed=int(size), transcendentals=int(transcendentals)
    )


def whole(shape):
    return pl.BlockSpec(shape, lambda *_: (0,) * len(shape))


def norm_stats(values):
    centered = values - jnp.mean(values, axis=-1, keepdims=True)
    inverse = lax.rsqrt(jnp.mean(centered * centered, axis=-1, keepdims=True) + EPS)
    return (centered * inverse, inverse)


def norm_back(gradient, normed, inverse, gain_row):
    scaled = gradient * gain_row
    return inverse * (
        scaled
        - jnp.mean(scaled, axis=-1, keepdims=True)
        - normed * jnp.mean(scaled * normed, axis=-1, keepdims=True)
    )


def turn(values, cosine, sine, sign):
    lane = lax.broadcasted_iota(jnp.int32, (values.shape[0], 128), 1) % HEAD_DIM
    parts = []
    for group in range(values.shape[1] // 128):
        part = values[:, group * 128 : group * 128 + 128]
        swapped = jnp.where(
            lane < HEAD_DIM // 2, pltpu.roll(part, 96, 1), pltpu.roll(part, 32, 1)
        )
        if sign > 0:
            parts.append(part * cosine + swapped * sine)
        else:
            parts.append(part * cosine - swapped * sine)
    return jnp.concatenate(parts, axis=1)


def tables_kernel(info_ref, lengths_ref, cos_ref, sin_ref, bias_ref):
    wide = cos_ref.shape[0]
    rows = wide - 2 * WINDOW
    base = info_ref[0] * rows
    total = info_ref[1]
    frame = base - WINDOW + lax.broadcasted_iota(jnp.int32, (wide, 128), 0)
    query = base + lax.broadcasted_iota(jnp.int32, (8, rows), 1)
    key_clip = jnp.full((wide, 128), -1, jnp.int32)
    begin = jnp.zeros((wide, 128), jnp.int32)
    query_clip = jnp.full((8, rows), -1, jnp.int32)

    def step(entry, carry):
        start, key_clip, begin, query_clip = carry
        inside = frame >= start
        key_clip = key_clip + inside.astype(jnp.int32)
        begin = jnp.where(inside, start, begin)
        query_clip = query_clip + (query >= start).astype(jnp.int32)
        return (start + lengths_ref[0, entry], key_clip, begin, query_clip)

    _, key_clip, begin, query_clip = lax.fori_loop(
        0, lengths_ref.shape[1], step, (jnp.int32(0), key_clip, begin, query_clip)
    )
    key_clip = jnp.where((frame >= 0) & (frame < total), key_clip, -1)
    lane = lax.broadcasted_iota(jnp.int32, (wide, 128), 1)
    frequency = jnp.exp(
        (lane % (HEAD_DIM // 2)).astype(F32) * (-2.0 * math.log(10000.0) / HEAD_DIM)
    )
    angle = (frame - begin).astype(F32) * frequency
    sine = jnp.sin(angle)
    cos_ref[...] = jnp.cos(angle)
    sin_ref[...] = jnp.where(lane % HEAD_DIM < HEAD_DIM // 2, -sine, sine)
    span = 3 * WINDOW
    gap = lax.broadcasted_iota(jnp.int32, (span, 128), 0) - lax.broadcasted_iota(
        jnp.int32, (span, 128), 1
    )
    near = (gap >= 0) & (gap <= 2 * WINDOW)
    for block in range(rows // WINDOW):
        at = block * WINDOW
        same = key_clip[at : at + span] == query_clip[0:1, at : at + WINDOW]
        bias_ref[block] = jnp.where(near & same, 0.0, -1e30)


def tables_call(info, lengths, rows):
    wide = rows + 2 * WINDOW
    return pl.pallas_call(
        tables_kernel,
        out_shape=(
            jax.ShapeDtypeStruct((wide, 128), F32),
            jax.ShapeDtypeStruct((wide, 128), F32),
            jax.ShapeDtypeStruct((rows // WINDOW, 3 * WINDOW, 128), F32),
        ),
        in_specs=[
            pl.BlockSpec(memory_space=pltpu.SMEM),
            pl.BlockSpec(memory_space=pltpu.SMEM),
        ],
        compiler_params=params(),
        cost_estimate=cost(1e8, 2e6),
        name="tables",
    )(info, lengths)


def project_kernel(x_ref, gain_ref, shift_ref, cos_ref, sin_ref, weight_ref, a1_ref, out_ref):
    chunk = pl.program_id(0)
    rows = x_ref.shape[0]

    @pl.when(chunk == 0)
    def _():
        normed, _unused = norm_stats(x_ref[...].astype(F32))
        a1_ref[...] = (normed * gain_ref[0:1, :] + shift_ref[0:1, :]).astype(BF)

    projected = dot_nn(a1_ref[...], weight_ref[...])
    cosine = cos_ref[WINDOW : WINDOW + rows, :]
    sine = sin_ref[WINDOW : WINDOW + rows, :]

    @pl.when(chunk < 2)
    def _():
        out_ref[...] = (turn(projected, cosine, sine, 1) * HEAD_DIM**-0.5).astype(BF)

    @pl.when((chunk >= 2) & (chunk < 4))
    def _():
        out_ref[...] = turn(projected, cosine, sine, 1).astype(BF)

    @pl.when(chunk >= 4)
    def _():
        out_ref[...] = projected.astype(BF)


def project_call(x, gains, shifts, cosine, sine, weight):
    rows = x.shape[0]
    wide = cosine.shape[0]
    return pl.pallas_call(
        project_kernel,
        grid=(6,),
        out_shape=(
            jax.ShapeDtypeStruct((rows, D), BF),
            jax.ShapeDtypeStruct((rows, 3 * D), BF),
        ),
        in_specs=[
            whole((rows, D)),
            whole((2, D)),
            whole((2, D)),
            whole((wide, 128)),
            whole((wide, 128)),
            pl.BlockSpec((D, 512), lambda c: (0, c)),
        ],
        out_specs=(whole((rows, D)), pl.BlockSpec((rows, 512), lambda c: (0, c))),
        compiler_params=params(),
        cost_estimate=cost(2 * rows * D * 3 * D, 12e6),
        name="project",
    )(x, gains, shifts, cosine, sine, weight)


def rim_kernel(
    low_ref, high_ref, gain_ref, shift_ref, cos_ref, sin_ref, weight_ref, out_ref, a1_ref
):
    chunk = pl.program_id(0)
    wide = cos_ref.shape[0]

    @pl.when(chunk == 0)
    def _():
        for at, ref in ((0, low_ref), (WINDOW, high_ref)):
            normed, _unused = norm_stats(ref[...].astype(F32))
            a1_ref[at : at + WINDOW, :] = (
                normed * gain_ref[0:1, :] + shift_ref[0:1, :]
            ).astype(BF)

    projected = dot_nn(a1_ref[...], weight_ref[...])

    @pl.when(chunk < 2)
    def _():
        cosine = jnp.concatenate([cos_ref[:WINDOW, :], cos_ref[wide - WINDOW :, :]], axis=0)
        sine = jnp.concatenate([sin_ref[:WINDOW, :], sin_ref[wide - WINDOW :, :]], axis=0)
        out_ref[...] = turn(projected, cosine, sine, 1).astype(BF)

    @pl.when(chunk >= 2)
    def _():
        out_ref[...] = projected.astype(BF)


def rim_call(low, high, gains, shifts, cosine, sine, weight):
    wide = cosine.shape[0]
    return pl.pallas_call(
        rim_kernel,
        grid=(4,),
        out_shape=jax.ShapeDtypeStruct((2 * WINDOW, 2 * D), BF),
        in_specs=[
            whole((WINDOW, D)),
            whole((WINDOW, D)),
            whole((2, D)),
            whole((2, D)),
            whole((wide, 128)),
            whole((wide, 128)),
            pl.BlockSpec((D, 512), lambda c: (0, c + 2)),
        ],
        out_specs=pl.BlockSpec((2 * WINDOW, 512), lambda c: (0, c)),
        scratch_shapes=[pltpu.VMEM((2 * WINDOW, D), BF)],
        compiler_params=params(),
        cost_estimate=cost(2 * 256 * D * 2 * D, 6e6),
        name="rim",
    )(low, high, gains, shifts, cosine, sine, weight)


def stacked(block):
    owner = lax.broadcasted_iota(jnp.int32, block.shape, 1) // HEAD_DIM
    zero = jnp.zeros_like(block)
    return jnp.concatenate([jnp.where(owner == head, block, zero) for head in range(4)], axis=0)


def attend_kernel(
    q_ref,
    k_ref,
    v_ref,
    rim_k_ref,
    rim_v_ref,
    bias_ref,
    weight_ref,
    x_ref,
    gain_ref,
    shift_ref,
    scale_ref,
    o_ref,
    lse_ref,
    x1_ref,
    attn_ref,
    a2_ref,
    keys,
    values_t,
    mixed_t,
    total,
):
    quad = pl.program_id(0)
    rows = q_ref.shape[0]
    keys[0:WINDOW, :] = rim_k_ref[0:WINDOW, :]
    keys[WINDOW : WINDOW + rows, :] = k_ref[...]
    keys[WINDOW + rows :, :] = rim_k_ref[WINDOW:, :]
    values_t[:, 0:WINDOW] = rim_v_ref[0:WINDOW, :].T
    values_t[:, WINDOW : WINDOW + rows] = v_ref[...].T
    values_t[:, WINDOW + rows :] = rim_v_ref[WINDOW:, :].T
    for block in range(rows // WINDOW):
        at = block * WINDOW
        queries = stacked(q_ref[at : at + WINDOW, :])
        scores = dot_nt(keys[at : at + 3 * WINDOW, :], queries)
        bias = bias_ref[block]
        scores = scores + jnp.concatenate([bias] * 4, axis=1)
        top = jnp.max(scores, axis=0, keepdims=True)
        weights = jnp.exp(scores - top)
        total_row = jnp.sum(weights, axis=0, keepdims=True)
        weights = (weights * (1.0 / total_row)).astype(BF)
        log_row = top + jnp.log(total_row)
        for head in range(4):
            lanes = slice(head * WINDOW, head * WINDOW + WINDOW)
            lse_ref[0, head : head + 1, at : at + WINDOW] = log_row[:, lanes]
            feature = slice(head * HEAD_DIM, head * HEAD_DIM + HEAD_DIM)
            mixed_t[feature, at : at + WINDOW] = dot_nn(
                values_t[feature, at : at + 3 * WINDOW], weights[:, lanes]
            )
    mixed = mixed_t[...].T.astype(BF)
    o_ref[...] = mixed
    branch = dot_nn(mixed, weight_ref[...])

    @pl.when(quad == 0)
    def _():
        total[...] = branch

    @pl.when(quad > 0)
    def _():
        total[...] += branch

    @pl.when(quad == HEADS // 4 - 1)
    def _():
        attn = total[...]
        residual = x_ref[...].astype(F32) + attn * scale_ref[0:1, :]
        normed, _unused = norm_stats(residual)
        x1_ref[...] = residual
        attn_ref[...] = attn.astype(BF)
        a2_ref[...] = (normed * gain_ref[1:2, :] + shift_ref[1:2, :]).astype(BF)


def attend_call(qkv, rim, bias, weight, x, gains, shifts, scales):
    rows = x.shape[0]
    wide = rows + 2 * WINDOW
    row_spec = whole((rows, D))
    return pl.pallas_call(
        attend_kernel,
        grid=(HEADS // 4,),
        out_shape=(
            jax.ShapeDtypeStruct((rows, D), BF),
            jax.ShapeDtypeStruct((HEADS // 4, 8, rows), F32),
            jax.ShapeDtypeStruct((rows, D), F32),
            jax.ShapeDtypeStruct((rows, D), BF),
            jax.ShapeDtypeStruct((rows, D), BF),
        ),
        in_specs=[
            pl.BlockSpec((rows, QUAD), lambda h: (0, h)),
            pl.BlockSpec((rows, QUAD), lambda h: (0, h + 4)),
            pl.BlockSpec((rows, QUAD), lambda h: (0, h + 8)),
            pl.BlockSpec((2 * WINDOW, QUAD), lambda h: (0, h)),
            pl.BlockSpec((2 * WINDOW, QUAD), lambda h: (0, h + 4)),
            whole(bias.shape),
            pl.BlockSpec((QUAD, D), lambda h: (h, 0)),
            row_spec,
            whole((2, D)),
            whole((2, D)),
            whole((2, D)),
        ],
        out_specs=(
            pl.BlockSpec((rows, QUAD), lambda h: (0, h)),
            pl.BlockSpec((1, 8, rows), lambda h: (h, 0, 0)),
            row_spec,
            row_spec,
            row_spec,
        ),
        scratch_shapes=[
            pltpu.VMEM((wide, QUAD), BF),
            pltpu.VMEM((QUAD, wide), BF),
            pltpu.VMEM((QUAD, rows), F32),
            pltpu.VMEM((rows, D), F32),
        ],
        compiler_params=params(),
        cost_estimate=cost(8e9, 14e6, 3e6),
        name="attend",
    )(qkv, qkv, qkv, rim, rim, bias, weight, x, gains, shifts, scales)


def gated(gate, up, grad_hidden):
    sigmoid = 0.5 * jnp.tanh(0.5 * gate) + 0.5
    swish = gate * sigmoid
    hidden = swish * up
    grad_gate = grad_hidden * up * (sigmoid + swish * (1.0 - sigmoid))
    grad_up = grad_hidden * swish
    return (hidden.astype(BF), grad_gate.astype(BF), grad_up.astype(BF))


def feed_kernel(
    a2_ref,
    dy_ref,
    x1_ref,
    attn_ref,
    gain_ref,
    scale_ref,
    gate_w_ref,
    up_w_ref,
    shrink_w_ref,
    act_ref,
    dx1_ref,
    dattn_ref,
    small_ref,
    branch_grad,
    mlp,
    back,
):
    chunk = pl.program_id(0)

    @pl.when(chunk == 0)
    def _():
        branch_grad[...] = (dy_ref[...].astype(F32) * scale_ref[1:2, :]).astype(BF)

    a2 = a2_ref[...]
    gate = dot_nn(a2, gate_w_ref[...])
    up = dot_nn(a2, up_w_ref[...])
    grad_hidden = dot_nt(branch_grad[...], shrink_w_ref[...])
    hidden, grad_gate, grad_up = gated(gate, up, grad_hidden)
    branch = dot_nn(hidden, shrink_w_ref[...])
    back_part = dot_nt(grad_gate, gate_w_ref[...]) + dot_nt(grad_up, up_w_ref[...])

    @pl.when(chunk == 0)
    def _():
        mlp[...] = branch
        back[...] = back_part

    @pl.when(chunk > 0)
    def _():
        mlp[...] += branch
        back[...] += back_part

    @pl.when(chunk == pl.num_programs(0) - 1)
    def _():
        residual = x1_ref[...]
        grad_result = dy_ref[...].astype(F32)
        branch = mlp[...]
        act_ref[...] = (residual + branch * scale_ref[1:2, :]).astype(BF)
        small_ref[0:1, :] = jnp.sum(grad_result * branch, axis=0, keepdims=True)
        grad_normed = back[...]
        normed, inverse = norm_stats(residual)
        small_ref[1:2, :] = jnp.sum(grad_normed * normed, axis=0, keepdims=True)
        small_ref[2:3, :] = jnp.sum(grad_normed, axis=0, keepdims=True)
        grad_residual = grad_result + norm_back(grad_normed, normed, inverse, gain_ref[1:2, :])
        dx1_ref[...] = grad_residual
        small_ref[3:4, :] = jnp.sum(
            grad_residual * attn_ref[...].astype(F32), axis=0, keepdims=True
        )
        small_ref[4:8, :] = jnp.zeros((4, D), F32)
        dattn_ref[...] = (grad_residual * scale_ref[0:1, :]).astype(BF)


def feed_call(a2, dy, x1, attn, gains, scales, expand, shrink):
    rows = a2.shape[0]
    size = 512
    count = FF // size
    row_spec = whole((rows, D))
    return pl.pallas_call(
        feed_kernel,
        grid=(count,),
        out_shape=(
            jax.ShapeDtypeStruct((rows, D), BF),
            jax.ShapeDtypeStruct((rows, D), F32),
            jax.ShapeDtypeStruct((rows, D), BF),
            jax.ShapeDtypeStruct((8, D), F32),
        ),
        in_specs=[
            row_spec,
            row_spec,
            row_spec,
            row_spec,
            whole((2, D)),
            whole((2, D)),
            pl.BlockSpec((D, size), lambda f: (0, f)),
            pl.BlockSpec((D, size), lambda f: (0, f + count)),
            pl.BlockSpec((size, D), lambda f: (f, 0)),
        ],
        out_specs=(row_spec, row_spec, row_spec, whole((8, D))),
        scratch_shapes=[
            pltpu.VMEM((rows, D), BF),
            pltpu.VMEM((rows, D), F32),
            pltpu.VMEM((rows, D), F32),
        ],
        compiler_params=params(),
        cost_estimate=cost(2 * rows * D * FF * 6, 36e6, rows * FF),
        name="feed",
    )(a2, dy, x1, attn, gains, scales, expand, expand, shrink)


def slice_kernel(pieces, outer, info_ref, *refs):
    a2_refs = refs[: len(pieces)]
    dy_refs = refs[len(pieces) : 2 * len(pieces)]
    scale_ref, gate_w_ref, up_w_ref, shrink_w_ref = refs[2 * len(pieces) : 2 * len(pieces) + 4]
    send_ref, keep_ref, a2_all, dy_all, acc, acc_shrink, sems = refs[2 * len(pieces) + 4 :]
    rows = a2_all.shape[1]
    groups = a2_all.shape[0]
    for number, (slot, first, size) in enumerate(pieces):
        for kind, (sources, held) in enumerate(((a2_refs, a2_all), (dy_refs, dy_all))):
            pltpu.make_async_copy(
                sources[number],
                held.at[slot, pl.ds(first, size), :],
                sems.at[kind, slot],
            ).start()
    acc[...] = jnp.zeros_like(acc)
    acc_shrink[...] = jnp.zeros_like(acc_shrink)

    def step(slot, _):
        for kind, held in enumerate((a2_all, dy_all)):
            pltpu.make_async_copy(held.at[slot], held.at[slot], sems.at[kind, slot]).wait()
        a2 = a2_all[slot]
        branch_grad = (dy_all[slot].astype(F32) * scale_ref[1:2, :]).astype(BF)
        gate = dot_nn(a2, gate_w_ref[...])
        up = dot_nn(a2, up_w_ref[...])
        grad_hidden = dot_nt(branch_grad, shrink_w_ref[...])
        hidden, grad_gate, grad_up = gated(gate, up, grad_hidden)
        acc[...] += dot_tn(a2, jnp.concatenate([grad_gate, grad_up], axis=1))
        acc_shrink[...] += dot_tn(branch_grad, hidden)
        return 0

    lax.fori_loop(0, groups, step, 0)
    mine = info_ref[1]
    span = D // (2 * outer)
    for at in range(outer):
        for target, bit in ((send_ref, 1 - mine), (keep_ref, mine)):
            first = pl.multiple_of(at * 2 * span + bit * span, span)
            target[at, :, : 2 * HALF] = acc[pl.ds(first, span), :].astype(BF)
            target[at, :, 2 * HALF :] = acc_shrink[pl.ds(first, span), :].astype(BF)


def slice_call(info, a2_list, dy_list, scales, expand, shrink, rows, outer):
    pieces = []
    slot, first = 0, 0
    for piece in a2_list:
        pieces.append((slot, first, piece.shape[0]))
        first += piece.shape[0]
        if first == rows:
            slot, first = slot + 1, 0
    groups = slot
    span = D // (2 * outer)
    hbm = pl.BlockSpec(memory_space=pl.ANY)
    result = jax.ShapeDtypeStruct((outer, span, 3 * HALF), BF)
    out_spec = pl.BlockSpec((outer, span, 3 * HALF), lambda i, info: (0, 0, 0))
    return pl.pallas_call(
        functools.partial(slice_kernel, tuple(pieces), outer),
        grid_spec=pltpu.PrefetchScalarGridSpec(
            num_scalar_prefetch=1,
            grid=(1,),
            in_specs=[hbm] * (2 * len(pieces))
            + [
                pl.BlockSpec((2, D), lambda i, info: (0, 0)),
                pl.BlockSpec((D, HALF), lambda i, info: (0, info[0])),
                pl.BlockSpec((D, HALF), lambda i, info: (0, info[0] + FF // HALF)),
                pl.BlockSpec((HALF, D), lambda i, info: (info[0], 0)),
            ],
            out_specs=(out_spec, out_spec),
            scratch_shapes=[
                pltpu.VMEM((groups, rows, D), BF),
                pltpu.VMEM((groups, rows, D), BF),
                pltpu.VMEM((D, 2 * HALF), F32),
                pltpu.VMEM((D, HALF), F32),
                pltpu.SemaphoreType.DMA((2, groups)),
            ],
        ),
        out_shape=(result, result),
        compiler_params=params(),
        cost_estimate=cost(2 * groups * rows * D * HALF * 6, 22e6, groups * rows * HALF),
        name="slice_grads",
    )(info, *a2_list, *dy_list, scales, expand, expand, shrink)


def attend_back_kernel(
    info_ref,
    q_ref,
    k_ref,
    v_ref,
    rim_k_ref,
    rim_v_ref,
    bias_ref,
    cos_ref,
    sin_ref,
    lse_ref,
    o_ref,
    dattn_ref,
    weight_ref,
    dq_ref,
    dk_ref,
    dv_ref,
    low_ref,
    high_ref,
    send_ref,
    keep_ref,
    keys,
    values,
    keys_t,
    grad_q_t,
    grad_k,
    grad_v,
):
    rows = q_ref.shape[0]
    for held, own, rim in ((keys, k_ref, rim_k_ref), (values, v_ref, rim_v_ref)):
        held[0:WINDOW, :] = rim[0:WINDOW, :]
        held[WINDOW : WINDOW + rows, :] = own[...]
        held[WINDOW + rows :, :] = rim[WINDOW:, :]
    keys_t[...] = keys[...].T
    dattn = dattn_ref[...]
    grad_mixed = dot_nt(dattn, weight_ref[...]).astype(BF)
    outer = dot_tn(o_ref[...], dattn).astype(BF)
    for core in range(2):

        @pl.when(info_ref[2] == core)
        def _():
            for half in range(2):
                for target, bit in ((keep_ref, core), (send_ref, 1 - core)):
                    first = (2 * half + bit) * QUAD
                    target[half] = outer[:, first : first + QUAD]

    grad_k[...] = jnp.zeros_like(grad_k)
    grad_v[...] = jnp.zeros_like(grad_v)
    for block in range(rows // WINDOW):
        at = block * WINDOW
        span = slice(at, at + 3 * WINDOW)
        queries = stacked(q_ref[at : at + WINDOW, :])
        grad_out = stacked(grad_mixed[at : at + WINDOW, :])
        scores = dot_nt(keys[span, :], queries)
        log_row = jnp.concatenate(
            [lse_ref[0, head : head + 1, at : at + WINDOW] for head in range(4)], axis=1
        )
        bias = bias_ref[block]
        weights = jnp.exp(scores + jnp.concatenate([bias] * 4, axis=1) - log_row)
        grad_weights = dot_nt(values[span, :], grad_out)
        weighted = weights * grad_weights
        grad_scores = weighted - weights * jnp.sum(weighted, axis=0, keepdims=True)
        grad_scores = grad_scores.astype(BF)
        grad_v[span, :] += dot_nn(weights.astype(BF), grad_out)
        grad_k[span, :] += dot_nn(grad_scores, queries)
        for head in range(4):
            feature = slice(head * HEAD_DIM, head * HEAD_DIM + HEAD_DIM)
            grad_q_t[feature, at : at + WINDOW] = dot_nn(
                keys_t[feature, span], grad_scores[:, head * WINDOW : head * WINDOW + WINDOW]
            )
    own = slice(WINDOW, WINDOW + rows)
    cosine, sine = cos_ref[...], sin_ref[...]
    dq_ref[...] = turn(
        grad_q_t[...].T * HEAD_DIM**-0.5, cosine[own, :], sine[own, :], -1
    ).astype(BF)
    turned = turn(grad_k[...], cosine, sine, -1).astype(BF)
    grad_values = grad_v[...].astype(BF)
    dk_ref[...] = turned[own, :]
    dv_ref[...] = grad_values[own, :]
    low_ref[0] = turned[:WINDOW, :]
    low_ref[1] = grad_values[:WINDOW, :]
    high_ref[0] = turned[WINDOW + rows :, :]
    high_ref[1] = grad_values[WINDOW + rows :, :]


def attend_back_call(info, qkv, rim, bias, cosine, sine, lse, o, dattn, weight):
    rows = o.shape[0]
    wide = rows + 2 * WINDOW
    row_shape = jax.ShapeDtypeStruct((rows, D), BF)
    rim_shape = jax.ShapeDtypeStruct((2, WINDOW, D), BF)
    grad_shape = jax.ShapeDtypeStruct((2, D, QUAD), BF)
    row_spec = pl.BlockSpec((rows, QUAD), lambda h, info: (0, h))
    rim_spec = pl.BlockSpec((2, WINDOW, QUAD), lambda h, info: (0, 0, h))
    grad_spec = pl.BlockSpec((2, QUAD, QUAD), lambda h, info: (0, h, 0))
    return pl.pallas_call(
        attend_back_kernel,
        grid_spec=pltpu.PrefetchScalarGridSpec(
            num_scalar_prefetch=1,
            grid=(HEADS // 4,),
            in_specs=[
                row_spec,
                pl.BlockSpec((rows, QUAD), lambda h, info: (0, h + 4)),
                pl.BlockSpec((rows, QUAD), lambda h, info: (0, h + 8)),
                pl.BlockSpec((2 * WINDOW, QUAD), lambda h, info: (0, h)),
                pl.BlockSpec((2 * WINDOW, QUAD), lambda h, info: (0, h + 4)),
                whole(bias.shape),
                whole((wide, 128)),
                whole((wide, 128)),
                pl.BlockSpec((1, 8, rows), lambda h, info: (h, 0, 0)),
                row_spec,
                whole((rows, D)),
                pl.BlockSpec((QUAD, D), lambda h, info: (h, 0)),
            ],
            out_specs=(row_spec, row_spec, row_spec, rim_spec, rim_spec, grad_spec, grad_spec),
            scratch_shapes=[
                pltpu.VMEM((wide, QUAD), BF),
                pltpu.VMEM((wide, QUAD), BF),
                pltpu.VMEM((QUAD, wide), BF),
                pltpu.VMEM((QUAD, rows), F32),
                pltpu.VMEM((wide, QUAD), F32),
                pltpu.VMEM((wide, QUAD), F32),
            ],
        ),
        out_shape=(
            row_shape,
            row_shape,
            row_shape,
            rim_shape,
            rim_shape,
            grad_shape,
            grad_shape,
        ),
        compiler_params=params(),
        cost_estimate=cost(2e10, 20e6, 3e6),
        name="attend_back",
    )(info, qkv, qkv, qkv, rim, rim, bias, cosine, sine, lse, o, dattn, weight)


def project_back_kernel(
    info_ref,
    dq_ref,
    dk_ref,
    dv_ref,
    low_ref,
    high_ref,
    a1_ref,
    x_ref,
    dx1_ref,
    gain_ref,
    weight_ref,
    grad_ref,
    small_ref,
    send_ref,
    keep_ref,
    part,
    back,
):
    chunk = pl.program_id(0)
    rows = dq_ref.shape[0]
    lanes = pl.ds(pl.multiple_of((chunk % 2) * 512, 512), 512)

    @pl.when(chunk < 2)
    def _():
        part[...] = dq_ref[:, lanes]

    for kind, ref in ((0, dk_ref), (1, dv_ref)):

        @pl.when(chunk // 2 == kind + 1)
        def _():
            part[WINDOW : rows - WINDOW, :] = ref[WINDOW : rows - WINDOW, lanes]
            for at, rim in ((0, low_ref), (rows - WINDOW, high_ref)):
                part[at : at + WINDOW, :] = (
                    ref[at : at + WINDOW, lanes].astype(F32) + rim[kind, :, lanes].astype(F32)
                ).astype(BF)

    grad_part = part[...]
    back_part = dot_nt(grad_part, weight_ref[...])

    @pl.when(chunk == 0)
    def _():
        back[...] = back_part

    @pl.when(chunk > 0)
    def _():
        back[...] += back_part

    outer = dot_tn(a1_ref[...], grad_part).astype(BF)
    for core in range(2):

        @pl.when(info_ref[2] == core)
        def _():
            keep_ref[0, 0] = outer[:, core * QUAD : core * QUAD + QUAD]
            send_ref[0, 0] = outer[:, (1 - core) * QUAD : (1 - core) * QUAD + QUAD]

    @pl.when(chunk == pl.num_programs(0) - 1)
    def _():
        grad_normed = back[...]
        normed, inverse = norm_stats(x_ref[...].astype(F32))
        small_ref[0:1, :] = jnp.sum(grad_normed * normed, axis=0, keepdims=True)
        small_ref[1:2, :] = jnp.sum(grad_normed, axis=0, keepdims=True)
        small_ref[2:8, :] = jnp.zeros((6, D), F32)
        grad_ref[...] = (
            dx1_ref[...] + norm_back(grad_normed, normed, inverse, gain_ref[0:1, :])
        ).astype(BF)


def project_back_call(info, dq, dk, dv, low, high, a1, x, dx1, gains, weight):
    rows = x.shape[0]
    row_spec = whole((rows, D))
    rim_spec = whole((2, WINDOW, D))
    grad_shape = jax.ShapeDtypeStruct((3, 2, D, QUAD), BF)
    grad_spec = pl.BlockSpec((1, 1, D, QUAD), lambda c, info: (c // 2, c % 2, 0, 0))
    return pl.pallas_call(
        project_back_kernel,
        grid_spec=pltpu.PrefetchScalarGridSpec(
            num_scalar_prefetch=1,
            grid=(6,),
            in_specs=[
                row_spec,
                row_spec,
                row_spec,
                rim_spec,
                rim_spec,
                row_spec,
                row_spec,
                row_spec,
                whole((2, D)),
                pl.BlockSpec((D, 512), lambda c, info: (0, c)),
            ],
            out_specs=(row_spec, whole((8, D)), grad_spec, grad_spec),
            scratch_shapes=[pltpu.VMEM((rows, 512), BF), pltpu.VMEM((rows, D), F32)],
        ),
        out_shape=(
            jax.ShapeDtypeStruct((rows, D), BF),
            jax.ShapeDtypeStruct((8, D), F32),
            grad_shape,
            grad_shape,
        ),
        compiler_params=params(),
        cost_estimate=cost(4 * rows * D * 3 * D, 22e6),
        name="project_back",
    )(info, dq, dk, dv, low, high, a1, x, dx1, gains, weight)


def place_kernel(count, info_ref, *refs):
    first, second = refs[:count], refs[count : 2 * count]
    expand_ref, shrink_ref = refs[2 * count :]
    slot = info_ref[0]
    for flip in range(count):
        unit = slot ^ flip
        for half, ref in ((0, first[flip]), (1, second[flip])):
            at = unit * PART + half * HALF
            expand_ref[:, pl.ds(pl.multiple_of(at, HALF), HALF)] = ref[:, :HALF].astype(F32)
            expand_ref[:, pl.ds(pl.multiple_of(FF + at, HALF), HALF)] = ref[
                :, HALF : 2 * HALF
            ].astype(F32)
            shrink_ref[pl.ds(pl.multiple_of(at, HALF), HALF), :] = ref[:, 2 * HALF :].astype(F32).T


def place_call(info, first, second):
    rows = first[0].shape[0]
    vmem = pl.BlockSpec(memory_space=pltpu.VMEM)
    return pl.pallas_call(
        functools.partial(place_kernel, len(first)),
        in_specs=[pl.BlockSpec(memory_space=pltpu.SMEM)] + [vmem] * (2 * len(first)),
        out_shape=(
            jax.ShapeDtypeStruct((rows, 2 * FF), F32),
            jax.ShapeDtypeStruct((FF, rows), F32),
        ),
        compiler_params=params(),
        cost_estimate=cost(1e6, 10e6),
        name="place_feed",
    )(info, *first, *second)


def place_attend_kernel(count, info_ref, *refs):
    attend_ref, output_ref = refs[count:]
    slot = info_ref[0]
    for flip in range(count):
        at = (slot ^ flip) * QUAD
        for block in range(4):
            value = refs[flip][block].astype(F32)
            if block < 3:
                attend_ref[:, pl.ds(pl.multiple_of(block * D + at, QUAD), QUAD)] = value
            else:
                output_ref[:, pl.ds(pl.multiple_of(at, QUAD), QUAD)] = value


def place_attend_call(info, pieces):
    rows = pieces[0].shape[1]
    vmem = pl.BlockSpec(memory_space=pltpu.VMEM)
    return pl.pallas_call(
        functools.partial(place_attend_kernel, len(pieces)),
        in_specs=[pl.BlockSpec(memory_space=pltpu.SMEM)] + [vmem] * len(pieces),
        out_shape=(
            jax.ShapeDtypeStruct((rows, 3 * D), F32),
            jax.ShapeDtypeStruct((rows, D), F32),
        ),
        compiler_params=params(),
        cost_estimate=cost(1e6, 4e6),
        name="place_attend",
    )(info, *pieces)


def add_up(terms):
    total = terms[0].astype(F32)
    for term in terms[1:]:
        total = total + term.astype(F32)
    return total


class Links:
    def __init__(self):
        self.dp_size = lax.axis_size("dp")
        self.seq_size = lax.axis_size("seq")
        self.dp = lax.axis_index("dp")
        self.seq = lax.axis_index("seq")
        self.dp_bits = self.dp_size.bit_length() - 1
        self.seq_bits = self.seq_size.bit_length() - 1

    def swap(self, value, axis, bit):
        size = self.dp_size if axis == "dp" else self.seq_size
        return lax.ppermute(value, axis, [(i, i ^ (1 << bit)) for i in range(size)])

    def bit(self, axis, bit):
        return ((self.dp if axis == "dp" else self.seq) >> bit) & 1

    def halve(self, terms, names, name):
        dim = names.index(name)
        mine = self.bit(*name)
        other = add_up(
            [lax.dynamic_index_in_dim(term, 1 - mine, dim, keepdims=False) for term in terms]
        ).astype(BF)
        got = self.swap(other, *name)
        kept = [lax.dynamic_index_in_dim(term, mine, dim, keepdims=False) for term in terms]
        return (kept + [got], names[:dim] + names[dim + 1 :])

    def reduce(self, terms, names, order):
        for name in order:
            terms, names = self.halve(terms, names, name)
        total = add_up(terms)
        for bit in range(2, self.seq_bits):
            total = total + self.swap(total.astype(BF), "seq", bit).astype(F32)
        return total.astype(BF)


def body(
    frames,
    cotangent,
    lengths,
    attend_weight,
    output_weight,
    expand_weight,
    shrink_weight,
    norm_gains,
    norm_biases,
    layer_scales,
):
    rows = frames.shape[1]
    links = Links()
    x = frames.reshape(rows, D)
    dy = cotangent.reshape(rows, D)
    core = links.bit("seq", 0)
    member = links.seq & 3
    slot = links.bit("dp", 0) * 4 + member
    block_rows = D // links.dp_size

    def shifted(value, steps):
        count = links.seq_size
        pairs = [(i, i + steps) for i in range(count) if 0 <= i + steps < count]
        return lax.ppermute(value, "seq", pairs)

    def gathered(value):
        over_x = links.swap(value, "seq", 1)
        over_y = links.swap(value, "dp", 0)
        top = links.swap(over_x[: rows // 2], "dp", 0)
        bottom = links.swap(over_y[rows // 2 :], "seq", 1)
        mine = [value, over_x, over_y, top, bottom]
        return mine + [links.swap(piece, "seq", 0) for piece in mine]

    low_frames = shifted(x[rows - WINDOW :], 1)
    high_frames = shifted(x[:WINDOW], -1)
    dy_pieces = gathered(dy)

    table_info = jnp.stack([links.seq, jnp.int32(links.seq_size * rows)]).astype(jnp.int32)
    cosine, sine, bias = tables_call(table_info, lengths, rows)
    a1, qkv = project_call(x, norm_gains, norm_biases, cosine, sine, attend_weight)
    rim = rim_call(low_frames, high_frames, norm_gains, norm_biases, cosine, sine, attend_weight)
    o, lse, x1, attn, a2 = attend_call(
        qkv, rim, bias, output_weight, x, norm_gains, norm_biases, layer_scales
    )
    a2_pieces = gathered(a2)
    act, dx1, dattn, small_feed = feed_call(
        a2, dy, x1, attn, norm_gains, layer_scales, expand_weight, shrink_weight
    )

    zero = jnp.int32(0)
    info = jnp.stack([zero, zero, core]).astype(jnp.int32)
    dq, dk, dv, low, high, out_send, out_keep = attend_back_call(
        info, qkv, rim, bias, cosine, sine, lse, o, dattn, output_weight
    )
    from_low = shifted(high, 1)
    from_high = shifted(low, -1)
    input_gradient, small_first, qkv_send, qkv_keep = project_back_call(
        info, dq, dk, dv, from_low, from_high, a1, x, dx1, norm_gains, attend_weight
    )

    outer = links.dp_size // 4
    high_bits = [("dp", bit) for bit in range(links.dp_bits - 1, -1, -1)]
    feed_done = []
    for half in range(2):
        slice_info = jnp.stack([slot * 2 + half, links.bit("dp", 1)]).astype(jnp.int32)
        send, keep = slice_call(
            slice_info, a2_pieces, dy_pieces, layer_scales, expand_weight, shrink_weight, rows, outer
        )
        got = links.swap(send, "dp", 1)
        shape = (2,) * (links.dp_bits - 2) + (2, block_rows, 3 * HALF)
        names = [name for name in high_bits if name[1] != 1]
        order = [("dp", bit) for bit in range(2, links.dp_bits)]
        total = links.reduce([keep.reshape(shape), got.reshape(shape)], names, order)
        mine = links.bit("dp", 0)
        pieces = [lax.dynamic_index_in_dim(total, mine, 0, keepdims=False)]
        pieces.append(
            links.swap(lax.dynamic_index_in_dim(total, 1 - mine, 0, keepdims=False), "dp", 0)
        )
        over_x = [links.swap(piece, "seq", 1) for piece in pieces]
        four = pieces + over_x
        over_core = [links.swap(piece, "seq", 0) for piece in four]
        order_of = [0, 4, 2, 6, 1, 5, 3, 7]
        eight = four + over_core
        feed_done.append([eight[order_of.index(flip)] for flip in range(8)])
    slot_info = slot.reshape(1).astype(jnp.int32)
    expand_grad, shrink_grad = place_call(slot_info, feed_done[0], feed_done[1])

    def piece_of(array):
        return array.reshape((2,) + (2,) * links.dp_bits + (block_rows, QUAD))

    names = [("seq", 1)] + high_bits
    over_x = ("seq", 1)
    over_y = ("dp", 0)
    over_z = [("dp", bit) for bit in range(1, links.dp_bits)]
    orders = [
        [over_x, over_y] + over_z,
        [over_y, over_x] + over_z,
        over_z + [over_x, over_y],
        [over_x, over_y] + over_z,
    ]
    qkv_got = links.swap(qkv_send, "seq", 0)
    out_got = links.swap(out_send, "seq", 0)
    done = []
    for block in range(4):
        if block < 3:
            terms = [piece_of(qkv_keep[block]), piece_of(qkv_got[block])]
        else:
            terms = [piece_of(out_keep), piece_of(out_got)]
        done.append(links.reduce(terms, names, orders[block]))
    stack = jnp.stack(done)
    across = links.swap(stack, "seq", 1)
    four = [stack, None, across, None]
    four[1] = links.swap(stack, "seq", 0)
    four[3] = links.swap(across, "seq", 0)
    attend_grad, output_grad = place_attend_call(member.reshape(1).astype(jnp.int32), four)

    small = jnp.concatenate([small_feed[:4], small_first[:2], jnp.zeros((2, D), F32)], axis=0)
    for axis, count in (("seq", links.seq_bits), ("dp", links.dp_bits)):
        for bit in range(count):
            small = small + links.swap(small, axis, bit)
    small = lax.dynamic_slice_in_dim(small, links.dp * block_rows, block_rows, axis=1)
    gains_grad = jnp.stack([small[4], small[1]])
    biases_grad = jnp.stack([small[5], small[2]])
    scales_grad = jnp.stack([small[3], small[0]])
    return (
        act.reshape(frames.shape),
        input_gradient.reshape(frames.shape),
        attend_grad,
        output_grad,
        expand_grad,
        shrink_grad,
        gains_grad,
        biases_grad,
        scales_grad,
    )


def solution(mesh):
    in_specs = (
        P("dp", "seq", None),
        P("dp", "seq", None),
        P("dp", None),
        P(),
        P(),
        P(),
        P(),
        P(),
        P(),
        P(),
    )
    out_specs = (
        P("dp", "seq", None),
        P("dp", "seq", None),
        P("dp", None),
        P("dp", None),
        P("dp", None),
        P(None, "dp"),
        P(None, "dp"),
        P(None, "dp"),
        P(None, "dp"),
    )
    return jax.shard_map(body, mesh=mesh, in_specs=in_specs, out_specs=out_specs, check_vma=False)
```

time: 1080 us -> 433 us (0.40)
  waiting for transfers between devices: 732 us -> 158 us
  matrix products: 192 us -> 0 us
  Pallas kernels: 0 us -> 177 us
  other arithmetic: 64.2 us -> 11.5 us
  starting transfers between devices: 15.4 us -> 62.7 us
  local copies, waits for them, and re-layouts: 48.1 us -> 14.5 us
  between operations: 15.1 us -> 1.77 us
    reduce_scatter x3 -> x0, waiting for transfers between devices: 463 us -> none  [the longest x1 286 us: body(): lax.psum_scatter(expand_grad.astype(jnp.bfloat16), 'dp', scatter_dimensio...]
    dot_general x18 -> x0, matrix products: 192 us -> none  [the longest x1 20 us: attend_back(): jnp.einsum('qhd,khd->hqk', grad_heads, values, preferred_element_type=jnp...]
    unnamed x12 -> x0, waiting for transfers between devices: 186 us -> none
    pallas_call x0 -> x11, Pallas kernels: none -> 177 us  [the longest x2 49.5 us: slice_call(): pl.pallas_call(functools.partial(slice_kernel, tuple(pieces), outer), gri...]
    ppermute x4 -> x66, waiting for transfers between devices: 2.82 us -> 158 us  [the longest x62 158 us: swap(): return lax.ppermute(value, axis, [(i, i ^ 1 << bit) for i in range(size)])]
    psum x1 -> x0, waiting for transfers between devices: 80.1 us -> none  [body(): lax.psum(summed[0].astype(jnp.bfloat16), 'seq').astype(jnp.float32)]
    ppermute x4 -> x66, starting transfers between devices: 14.9 us -> 62.7 us  [the longest x62 52.6 us: swap(): return lax.ppermute(value, axis, [(i, i ^ 1 << bit) for i in range(size)])]
    unnamed x105 -> x70, local copies, waits for them, and re-layouts: 39.4 us -> 6.1 us
  transfers between devices with their start and end apart: 12 -> 66, of which waited for: 8 -> 22; matrix products, arithmetic and copies ran while one was open for 15% -> 4% of each run, Pallas kernels for 0% -> 22%
where the time goes in v1:
time: 433 us; the launch traced here: 425 us
  Pallas kernels  177 us (41%)
  waiting for transfers between devices  158 us (36%)
  starting transfers between devices  62.7 us (14%)
  local copies, waits for them, and re-layouts  14.5 us (3%)
  other arithmetic  11.5 us (3%)
    ppermute x62, waiting for transfers between devices, swap(): return lax.ppermute(value, axis, [(i, i ^ 1 << bit) for i in range(size)])  158 us
    ppermute x62, starting transfers between devices, swap(): return lax.ppermute(value, axis, [(i, i ^ 1 << bit) for i in range(size)])  52.6 us
    pallas_call x2, Pallas kernels, slice_call(): pl.pallas_call(functools.partial(slice_kernel, tuple(pieces), outer), gri...  49.5 us
    pallas_call x1, Pallas kernels, feed_call(): pl.pallas_call(feed_kernel, grid=(count,), out_shape=(jax.ShapeDtypeStruc...  40 us
    pallas_call x1, Pallas kernels, attend_back_call(): pl.pallas_call(attend_back_kernel, grid_spec=pltpu.PrefetchScalarGridSpec...  20.4 us
    pallas_call x1, Pallas kernels, project_back_call(): pl.pallas_call(project_back_kernel, grid_spec=pltpu.PrefetchScalarGridSpe...  19.1 us
    pallas_call x1, Pallas kernels, attend_call(): pl.pallas_call(attend_kernel, grid=(HEADS // 4,), out_shape=(jax.ShapeDty...  16.4 us
    pallas_call x1, Pallas kernels, project_call(): pl.pallas_call(project_kernel, grid=(6,), out_shape=(jax.ShapeDtypeStruct...  11.5 us
  transfers between devices with their start and end apart: 66, of which 22 were waited for; matrix products, arithmetic and copies ran while one was open for 4% of the time, Pallas kernels for 22%

profile of v1, /device:TPU:0, one launch (start us, length us, event | category | flops | bytes accessed | tf_op | source)
XLA Modules:
  0.0 425.3 jit_solution(11377077252802336220)
XLA Ops:
  6.6 6.5 %tables.1 = (f32[768,128]{1,0:T(8,128)}, f32[768,128]{1,0:T(8,128)}, f32[4,384,128]{2,1,0:T(8,128)}) custom-call(s32[2]{0:T(128)} %pad_add_fusion.info_ref, s32[1,17]{1,0:T(1,128)} %lengths_ref.1), custom_call_target="tpu_custom_call" | custom-call | flops 100000000 | bytes 2000000 | tf_op jit(solution)/shard_map/tables/pallas_call | solution.py:126
  13.0 11.5 %project.1 = (bf16[512,1024]{1,0:T(8,128)(2,1)}, bf16[512,3072]{1,0:T(8,128)(2,1)}) custom-call(bf16[512,1024]{1,0:T(8,128)(2,1)} %bitcast.290, f32[2,1024]{1,0:T(2,128)} %gain_ref.9, f32[2,1024]{1,0:T(2,128)} %shift_ref.5, f32[768,128]{1,0:T(8,128)} %get-tuple-element.42.cos_ref, f32[768,128]{1,0:T(8,128)} %get-tuple-element.43.sin_ref, ...), custom_call_target="tpu_custom_call" | custom-call | flops 3221225472 | bytes 12000000 | tf_op jit(solution)/shard_map/project/pallas_call | solution.py:172
  26.0 6.2 %rim.1.rim_k_ref.rim_v_ref = bf16[256,2048]{1,0:T(8,128)(2,1)} custom-call(bf16[128,1024]{1,0:T(8,128)(2,1)} %copy-done.13, bf16[128,1024]{1,0:T(8,128)(2,1)} %copy-done.14, f32[2,1024]{1,0:T(2,128)} %gain_ref.9, f32[2,1024]{1,0:T(2,128)} %shift_ref.5, f32[768,128]{1,0:T(8,128)} %get-tuple-element.42.cos_ref, f32[768,128]{1,0:T(8,128)} %get-tuple-element.43.sin_ref, ...), custom_call_target="tpu_custom_call" | custom-call | flops 1073741824 | bytes 6000000 | tf_op jit(solution)/shard_map/rim/pallas_call | solution.py:223
  32.2 16.4 %attend.1 = (bf16[512,1024]{1,0:T(8,128)(2,1)}, f32[4,8,512]{2,1,0:T(8,128)}, f32[512,1024]{1,0:T(8,128)}, bf16[512,1024]{1,0:T(8,128)(2,1)}, bf16[512,1024]{1,0:T(8,128)(2,1)}) custom-call(bf16[512,3072]{1,0:T(8,128)(2,1)} %get-tuple-element.44.q_ref.k_ref.v_ref, bf16[512,3072]{1,0:T(8,128)(2,1)} %get-tuple-element.44.q_ref.k_ref.v_ref, ...), custom_call_target="tpu_custom_call" | custom-call | flops 8000000000 | bytes 14000000 | tf_op jit(solution)/shard_map/attend/pallas_call | solution.py:324
  48.6 40.0 %feed.1 = (bf16[512,1024]{1,0:T(8,128)(2,1)}, f32[512,1024]{1,0:T(8,128)}, bf16[512,1024]{1,0:T(8,128)(2,1)}, f32[8,1024]{1,0:T(8,128)}) custom-call(bf16[512,1024]{1,0:T(8,128)(2,1)} %get-tuple-element.46.a2_ref.refs_0_, bf16[512,1024]{1,0:T(8,128)(2,1)} %bitcast.4.dy_ref.refs_10_, f32[512,1024]{1,0:T(8,128)} %get-tuple-element.47.x1_ref, ...), custom_call_target="tpu_custom_call" | custom-call | flops 25769803776 | bytes 36000000 | tf_op jit(solution)/shard_map/feed/pallas_call | solution.py:442
  88.6 20.4 %attend_back.1 = (bf16[512,1024]{1,0:T(8,128)(2,1)}, bf16[512,1024]{1,0:T(8,128)(2,1)}, bf16[512,1024]{1,0:T(8,128)(2,1)}, bf16[2,128,1024]{2,1,0:T(8,128)(2,1)}...) custom-call(s32[3]{0:T(128)} %stack.55.info_ref, ...), custom_call_target="tpu_custom_call" | custom-call | flops 20000000000 | bytes 20000000 | tf_op jit(solution)/shard_map/attend_back/pallas_call | solution.py:649
  109.0 5.2 %collective-permute-start.2 = (bf16[2,128,1024]{2,1,0:T(8,128)(2,1)}, bf16[2,128,1024]{2,1,0:T(8,128)(2,1)S(1)}, u32[]{:S(2)}, u32[]{:S(2)}) collective-permute-start(bf16[2,128,1024]{2,1,0:T(8,128)(2,1)} %get-tuple-element.56), channel_id=1, source_target_pairs={{0,1},{1,2},{2,3},{4,5},{5,6},{6,7},{8,9},{9,10},{10,11},{12,13},{... | collective-permute-start | bytes 1572872 | tf_op jit(solution)/shard_map/ppermute | solution.py:925
  120.6 19.1 %project_back.1 = (bf16[512,1024]{1,0:T(8,128)(2,1)}, f32[8,1024]{1,0:T(8,128)}, bf16[3,2,1024,256]{3,2,1,0:T(8,128)(2,1)}, bf16[3,2,1024,256]{3,2,1,0:T(8,128)(2,1)}) custom-call(s32[3]{0:T(128)} %stack.55.info_ref, bf16[512,1024]{1,0:T(8,128)(2,1)} %get-tuple-element.53.dq_ref, bf16[512,1024]{1,0:T(8,128)(2,1)} %get-tuple-element.54.dk_ref, ...), custom_call_target="tpu_custom_call" | custom-call | flops 6442450944 | bytes 22000000 | tf_op jit(solution)/shard_map/project_back/pallas_call | solution.py:767
  140.5 12.3 %collective-permute-start.61 = (f32[8,1024]{1,0:T(8,128)S(1)}, f32[8,1024]{1,0:T(8,128)S(1)}, u32[]{:S(2)}, u32[]{:S(2)}) collective-permute-start(f32[8,1024]{1,0:T(8,128)S(1)} %maximum_maximum_fusion), channel_id=1, source_target_pairs={{0,1},{1,0},{2,3},{3,2},{4,5},{5,4},{6,7},{7,6},{8,9},{9,8},{10,11... | collective-permute-start | bytes 98312 | tf_op jit(solution)/shard_map/ppermute | solution.py:877
  156.4 23.7 %collective-permute-done.62 = f32[8,1024]{1,0:T(8,128)S(1)} collective-permute-done((f32[8,1024]{1,0:T(8,128)S(1)}, f32[8,1024]{1,0:T(8,128)S(1)}, u32[]{:S(2)}, u32[]{:S(2)}) %collective-permute-start.62) | collective-permute-done | bytes 32800 | tf_op jit(solution)/shard_map/ppermute | solution.py:877
  189.2 21.2 %collective-permute-done.26.refs_2_ = bf16[512,1024]{1,0:T(8,128)(2,1)} collective-permute-done((bf16[512,1024]{1,0:T(8,128)(2,1)}, bf16[512,1024]{1,0:T(8,128)(2,1)}, u32[]{:S(2)}, u32[]{:S(2)}) %collective-permute-start.26) | collective-permute-done | bytes 1048608 | tf_op jit(solution)/shard_map/ppermute | solution.py:877
  214.0 5.7 %collective-permute-done.36.refs_13_ = bf16[256,1024]{1,0:T(8,128)(2,1)S(1)} collective-permute-done((bf16[256,1024]{1,0:T(8,128)(2,1)S(1)}, bf16[256,1024]{1,0:T(8,128)(2,1)S(1)}, u32[]{:S(2)}, u32[]{:S(2)}) %collective-permute-start.36) | collective-permute-done | bytes 524320 | tf_op jit(solution)/shard_map/ppermute | solution.py:877
  223.2 7.9 %collective-permute-done.27.refs_3_ = bf16[256,1024]{1,0:T(8,128)(2,1)} collective-permute-done((bf16[256,1024]{1,0:T(8,128)(2,1)}, bf16[256,1024]{1,0:T(8,128)(2,1)}, u32[]{:S(2)}, u32[]{:S(2)}) %collective-permute-start.27) | collective-permute-done | bytes 524320 | tf_op jit(solution)/shard_map/ppermute | solution.py:877
  243.9 24.4 %slice_grads.2 = (bf16[2,256,768]{2,1,0:T(8,128)(2,1)}, bf16[2,256,768]{2,1,0:T(8,128)(2,1)}) custom-call(s32[2]{0:T(128)} %get-tuple-element.93.info_ref, bf16[512,1024]{1,0:T(8,128)(2,1)} %get-tuple-element.46.a2_ref.refs_0_, bf16[512,1024]{1,0:T(8,128)(2,1)} %copy-done.2, bf16[512,1024]{1,0:T(8,128)(2,1)} %collective-permute-done.26.refs_2_, ...), custom_call_target="tpu_custom_call" | custom-call | flops 12884901888 | bytes 22000000 | tf_op jit(solution)/shard_map/slice_grads/pallas_call | solution.py:527
  269.9 25.1 %slice_grads.3 = (bf16[2,256,768]{2,1,0:T(8,128)(2,1)}, bf16[2,256,768]{2,1,0:T(8,128)(2,1)}) custom-call(s32[2]{0:T(128)} %get-tuple-element.94.info_ref, bf16[512,1024]{1,0:T(8,128)(2,1)} %get-tuple-element.46.a2_ref.refs_0_, bf16[512,1024]{1,0:T(8,128)(2,1)} %copy-done.2, bf16[512,1024]{1,0:T(8,128)(2,1)} %collective-permute-done.26.refs_2_, ...), custom_call_target="tpu_custom_call" | custom-call | flops 12884901888 | bytes 22000000 | tf_op jit(solution)/shard_map/slice_grads/pallas_call | solution.py:527
  303.3 11.8 %collective-permute-done.21 = bf16[128,256]{1,0:T(8,128)(2,1)S(1)} collective-permute-done((bf16[128,256]{1,0:T(8,128)(2,1)S(1)}, bf16[128,256]{1,0:T(8,128)(2,1)S(1)}, u32[]{:S(2)}, u32[]{:S(2)}) %collective-permute-start.21) | collective-permute-done | bytes 65568 | tf_op jit(solution)/shard_map/ppermute | solution.py:877
  316.2 8.4 %collective-permute-done.52 = bf16[2,256,768]{2,1,0:T(8,128)(2,1)S(1)} collective-permute-done((bf16[2,256,768]{2,1,0:T(8,128)(2,1)}, bf16[2,256,768]{2,1,0:T(8,128)(2,1)S(1)}, u32[]{:S(2)}, u32[]{:S(2)}) %collective-permute-start.52) | collective-permute-done | bytes 786464 | tf_op jit(solution)/shard_map/ppermute | solution.py:877
  331.9 11.7 %collective-permute-done.53 = bf16[2,128,768]{2,1,0:T(8,128)(2,1)S(1)} collective-permute-done((bf16[2,128,768]{2,1,0:T(8,128)(2,1)S(1)}, bf16[2,128,768]{2,1,0:T(8,128)(2,1)S(1)}, u32[]{:S(2)}, u32[]{:S(2)}) %collective-permute-start.53) | collective-permute-done | bytes 393248 | tf_op jit(solution)/shard_map/ppermute | solution.py:877
  350.5 9.5 %collective-permute-done.14 = bf16[2,2,128,256]{3,2,1,0:T(8,128)(2,1)S(1)} collective-permute-done((bf16[2,2,128,256]{3,2,1,0:T(8,128)(2,1)S(1)}, bf16[2,2,128,256]{3,2,1,0:T(8,128)(2,1)S(1)}, u32[]{:S(2)}, u32[]{:S(2)}) %collective-permute-start.14) | collective-permute-done | bytes 262176 | tf_op jit(solution)/shard_map/ppermute | solution.py:877
  362.5 6.4 %collective-permute-done.15 = bf16[2,128,256]{2,1,0:T(8,128)(2,1)S(1)} collective-permute-done((bf16[2,128,256]{2,1,0:T(8,128)(2,1)S(1)}, bf16[2,128,256]{2,1,0:T(8,128)(2,1)S(1)}, u32[]{:S(2)}, u32[]{:S(2)}) %collective-permute-start.15) | collective-permute-done | bytes 131104 | tf_op jit(solution)/shard_map/ppermute | solution.py:877
  379.4 5.6 %collective-permute-done.12 = bf16[128,256]{1,0:T(8,128)(2,1)S(1)} collective-permute-done((bf16[128,256]{1,0:T(8,128)(2,1)S(1)}, bf16[128,256]{1,0:T(8,128)(2,1)S(1)}, u32[]{:S(2)}, u32[]{:S(2)}) %collective-permute-start.12) | collective-permute-done | bytes 65568 | tf_op jit(solution)/shard_map/ppermute | solution.py:877
  385.0 5.3 %collective-permute-done.8 = bf16[128,256]{1,0:T(8,128)(2,1)S(1)} collective-permute-done((bf16[128,256]{1,0:T(8,128)(2,1)S(1)}, bf16[128,256]{1,0:T(8,128)(2,1)S(1)}, u32[]{:S(2)}, u32[]{:S(2)}) %collective-permute-start.8) | collective-permute-done | bytes 65568 | tf_op jit(solution)/shard_map/ppermute | solution.py:877
  393.6 9.9 %collective-permute-done.55.refs_10_ = bf16[128,768]{1,0:T(8,128)(2,1)S(1)} collective-permute-done((bf16[128,768]{1,0:T(8,128)(2,1)S(1)}, bf16[128,768]{1,0:T(8,128)(2,1)S(1)}, u32[]{:S(2)}, u32[]{:S(2)}) %collective-permute-start.55) | collective-permute-done | bytes 196640 | tf_op jit(solution)/shard_map/ppermute | solution.py:877
  406.1 5.2 %collective-permute-done.50.refs_6_ = bf16[128,768]{1,0:T(8,128)(2,1)S(1)} collective-permute-done((bf16[128,768]{1,0:T(8,128)(2,1)S(1)}, bf16[128,768]{1,0:T(8,128)(2,1)S(1)}, u32[]{:S(2)}, u32[]{:S(2)}) %collective-permute-start.50) | collective-permute-done | bytes 196640 | tf_op jit(solution)/shard_map/ppermute | solution.py:877
  (239 shorter events, 104.1 us)
Async XLA Ops:
  1.7 22.8 %collective-permute-start = (bf16[128,1024]{1,0:T(8,128)(2,1)S(1)}, bf16[128,1024]{1,0:T(8,128)(2,1)S(1)}, u32[]{:S(2)}, u32[]{:S(2)}) collective-permute-start(bf16[128,1024]{1,0:T(8,128)(2,1)S(1)} %get-tuple-element.82), channel_id=1, source_target_pairs={{0,1},{1,2},{2,3},{4,5},{5,6},{6,7},{8,9},{9,10},{10,11},{12,13},{... | collective-permute-start | bytes 786440 | tf_op jit(solution)/shard_map/ppermute | solution.py:925
  4.1 20.5 %collective-permute-start.1 = (bf16[128,1024]{1,0:T(8,128)(2,1)S(1)}, bf16[128,1024]{1,0:T(8,128)(2,1)S(1)}, u32[]{:S(2)}, u32[]{:S(2)}) collective-permute-start(bf16[128,1024]{1,0:T(8,128)(2,1)S(1)} %get-tuple-element.81), channel_id=1, source_target_pairs={{1,0},{2,1},{3,2},{5,4},{6,5},{7,6},{9,8},{10,9},{11,10},{13,12},{... | collective-permute-start | bytes 786440 | tf_op jit(solution)/shard_map/ppermute | solution.py:925
  115.5 69.1 %collective-permute-start.34 = (bf16[512,1024]{1,0:T(8,128)(2,1)}, bf16[512,1024]{1,0:T(8,128)(2,1)S(1)}, u32[]{:S(2)}, u32[]{:S(2)}) collective-permute-start(bf16[512,1024]{1,0:T(8,128)(2,1)} %bitcast.4.dy_ref.refs_10_), channel_id=1, source_target_pairs={{0,2},{1,3},{2,0},{3,1},{4,6},{5,7},{6,4},{7,5},{8,10},{9,11},{10,... | collective-permute-start | bytes 3145736 | tf_op jit(solution)/shard_map/ppermute | solution.py:877
  119.6 65.0 %collective-permute-start.17 = (bf16[2,1024,256]{2,1,0:T(8,128)(2,1)}, bf16[2,1024,256]{2,1,0:T(8,128)(2,1)}, u32[]{:S(2)}, u32[]{:S(2)}) collective-permute-start(bf16[2,1024,256]{2,1,0:T(8,128)(2,1)} %get-tuple-element.64), channel_id=1, source_target_pairs={{0,1},{1,0},{2,3},{3,2},{4,5},{5,4},{6,7},{7,6},{8,9},{9,8},{10,11... | collective-permute-start | bytes 3145736 | tf_op jit(solution)/shard_map/ppermute | solution.py:877
  152.8 33.6 %collective-permute-start.35 = (bf16[512,1024]{1,0:T(8,128)(2,1)}, bf16[512,1024]{1,0:T(8,128)(2,1)S(1)}, u32[]{:S(2)}, u32[]{:S(2)}) collective-permute-start(bf16[512,1024]{1,0:T(8,128)(2,1)} %bitcast.4.dy_ref.refs_10_), channel_id=1, source_target_pairs={{0,4},{4,0},{8,12},{12,8},{16,20},{20,16},{24,28},{28,24},{1,5},{5... | collective-permute-start | bytes 3145736 | tf_op jit(solution)/shard_map/ppermute | solution.py:877
  154.3 33.7 %collective-permute-start.25 = (bf16[512,1024]{1,0:T(8,128)(2,1)}, bf16[512,1024]{1,0:T(8,128)(2,1)S(1)}, u32[]{:S(2)}, u32[]{:S(2)}) collective-permute-start(bf16[512,1024]{1,0:T(8,128)(2,1)} %get-tuple-element.46.a2_ref.refs_0_), channel_id=1, source_target_pairs={{0,2},{1,3},{2,0},{3,1},{4,6},{5,7},{6,4},{7,5},{8,10},{9,11},{10,... | collective-permute-start | bytes 3145736 | tf_op jit(solution)/shard_map/ppermute | solution.py:877
  154.4 25.7 %collective-permute-start.62 = (f32[8,1024]{1,0:T(8,128)S(1)}, f32[8,1024]{1,0:T(8,128)S(1)}, u32[]{:S(2)}, u32[]{:S(2)}) collective-permute-start(f32[8,1024]{1,0:T(8,128)S(1)} %fusion.33), channel_id=1, source_target_pairs={{0,2},{1,3},{2,0},{3,1},{4,6},{5,7},{6,4},{7,5},{8,10},{9,11},{10,... | collective-permute-start | bytes 98312 | tf_op jit(solution)/shard_map/ppermute | solution.py:877
  184.0 26.4 %collective-permute-start.26 = (bf16[512,1024]{1,0:T(8,128)(2,1)}, bf16[512,1024]{1,0:T(8,128)(2,1)}, u32[]{:S(2)}, u32[]{:S(2)}) collective-permute-start(bf16[512,1024]{1,0:T(8,128)(2,1)} %get-tuple-element.46.a2_ref.refs_0_), channel_id=1, source_target_pairs={{0,4},{4,0},{8,12},{12,8},{16,20},{20,16},{24,28},{28,24},{1,5},{5... | collective-permute-start | bytes 3145736 | tf_op jit(solution)/shard_map/ppermute | solution.py:877
  184.5 28.9 %collective-permute-start.38 = (bf16[512,1024]{1,0:T(8,128)(2,1)}, bf16[512,1024]{1,0:T(8,128)(2,1)}, u32[]{:S(2)}, u32[]{:S(2)}) collective-permute-start(bf16[512,1024]{1,0:T(8,128)(2,1)} %bitcast.4.dy_ref.refs_10_), channel_id=1, source_target_pairs={{0,1},{1,0},{2,3},{3,2},{4,5},{5,4},{6,7},{7,6},{8,9},{9,8},{10,11... | collective-permute-start | bytes 3145736 | tf_op jit(solution)/shard_map/ppermute | solution.py:877
  184.6 28.9 %collective-permute-start.29 = (bf16[512,1024]{1,0:T(8,128)(2,1)}, bf16[512,1024]{1,0:T(8,128)(2,1)}, u32[]{:S(2)}, u32[]{:S(2)}) collective-permute-start(bf16[512,1024]{1,0:T(8,128)(2,1)} %get-tuple-element.46.a2_ref.refs_0_), channel_id=1, source_target_pairs={{0,1},{1,0},{2,3},{3,2},{4,5},{5,4},{6,7},{7,6},{8,9},{9,8},{10,11... | collective-permute-start | bytes 3145736 | tf_op jit(solution)/shard_map/ppermute | solution.py:877
  186.4 33.3 %collective-permute-start.36 = (bf16[256,1024]{1,0:T(8,128)(2,1)S(1)}, bf16[256,1024]{1,0:T(8,128)(2,1)S(1)}, u32[]{:S(2)}, u32[]{:S(2)}) collective-permute-start(bf16[256,1024]{1,0:T(8,128)(2,1)S(1)} %slice.93), channel_id=1, source_target_pairs={{0,4},{4,0},{8,12},{12,8},{16,20},{20,16},{24,28},{28,24},{1,5},{5... | collective-permute-start | bytes 1572872 | tf_op jit(solution)/shard_map/ppermute | solution.py:877
  188.0 32.5 %collective-permute-start.18 = (bf16[2,2,2,128,256]{4,3,2,1,0:T(8,128)(2,1)S(1)}, bf16[2,2,2,128,256]{4,3,2,1,0:T(8,128)(2,1)S(1)}, u32[]{:S(2)}, u32[]{:S(2)}) collective-permute-start(bf16[2,2,2,128,256]{4,3,2,1,0:T(8,128)(2,1)S(1)} %fusion.5), channel_id=1, source_target_pairs={{0,2},{1,3},{2,0},{3,1},{4,6},{5,7},{6,4},{7,5},{8,10},{9,11},{10,... | collective-permute-start | bytes 1572872 | tf_op jit(solution)/shard_map/ppermute | solution.py:877
  213.5 21.7 %collective-permute-start.39 = (bf16[512,1024]{1,0:T(8,128)(2,1)S(1)}, bf16[512,1024]{1,0:T(8,128)(2,1)}, u32[]{:S(2)}, u32[]{:S(2)}) collective-permute-start(bf16[512,1024]{1,0:T(8,128)(2,1)S(1)} %collective-permute-done.34.refs_11_), channel_id=1, source_target_pairs={{0,1},{1,0},{2,3},{3,2},{4,5},{5,4},{6,7},{7,6},{8,9},{9,8},{10,11... | collective-permute-start | bytes 3145736 | tf_op jit(solution)/shard_map/ppermute | solution.py:877
  240.6 85.0 %collective-permute-start.4 = (bf16[3,2,1024,256]{3,2,1,0:T(8,128)(2,1)}, bf16[3,2,1024,256]{3,2,1,0:T(8,128)(2,1)}, u32[]{:S(2)}, u32[]{:S(2)}) collective-permute-start(bf16[3,2,1024,256]{3,2,1,0:T(8,128)(2,1)} %get-tuple-element.62), channel_id=1, source_target_pairs={{0,1},{1,0},{2,3},{3,2},{4,5},{5,4},{6,7},{7,6},{8,9},{9,8},{10,11... | collective-permute-start | bytes 9437192 | tf_op jit(solution)/shard_map/ppermute | solution.py:877
  241.1 58.9 %collective-permute-start.64 = (f32[8,1024]{1,0:T(8,128)}, f32[8,1024]{1,0:T(8,128)}, u32[]{:S(2)}, u32[]{:S(2)}) collective-permute-start(f32[8,1024]{1,0:T(8,128)} %add.935), channel_id=1, source_target_pairs={{0,8},{4,12},{8,0},{12,4},{16,24},{20,28},{24,16},{28,20},{1,9},{5... | collective-permute-start | bytes 98312 | tf_op jit(solution)/shard_map/ppermute | solution.py:877
  242.6 52.9 %collective-permute-start.20 = (bf16[2,128,256]{2,1,0:T(8,128)(2,1)S(1)}, bf16[2,128,256]{2,1,0:T(8,128)(2,1)}, u32[]{:S(2)}, u32[]{:S(2)}) collective-permute-start(bf16[2,128,256]{2,1,0:T(8,128)(2,1)S(1)} %fusion.12), channel_id=1, source_target_pairs={{0,8},{4,12},{8,0},{12,4},{16,24},{20,28},{24,16},{28,20},{1,9},{5... | collective-permute-start | bytes 393224 | tf_op jit(solution)/shard_map/ppermute | solution.py:877
  268.3 30.9 %collective-permute-start.43 = (bf16[2,256,768]{2,1,0:T(8,128)(2,1)}, bf16[2,256,768]{2,1,0:T(8,128)(2,1)S(1)}, u32[]{:S(2)}, u32[]{:S(2)}) collective-permute-start(bf16[2,256,768]{2,1,0:T(8,128)(2,1)} %get-tuple-element.68), channel_id=1, source_target_pairs={{0,8},{4,12},{8,0},{12,4},{16,24},{20,28},{24,16},{28,20},{1,9},{5... | collective-permute-start | bytes 2359304 | tf_op jit(solution)/shard_map/ppermute | solution.py:877
  295.0 29.6 %collective-permute-start.52 = (bf16[2,256,768]{2,1,0:T(8,128)(2,1)}, bf16[2,256,768]{2,1,0:T(8,128)(2,1)S(1)}, u32[]{:S(2)}, u32[]{:S(2)}) collective-permute-start(bf16[2,256,768]{2,1,0:T(8,128)(2,1)} %get-tuple-element.70), channel_id=1, source_target_pairs={{0,8},{4,12},{8,0},{12,4},{16,24},{20,28},{24,16},{28,20},{1,9},{5... | collective-permute-start | bytes 2359304 | tf_op jit(solution)/shard_map/ppermute | solution.py:877
  299.3 26.1 %collective-permute-start.44 = (bf16[2,128,768]{2,1,0:T(8,128)(2,1)S(1)}, bf16[2,128,768]{2,1,0:T(8,128)(2,1)S(1)}, u32[]{:S(2)}, u32[]{:S(2)}) collective-permute-start(bf16[2,128,768]{2,1,0:T(8,128)(2,1)S(1)} %fusion.10), channel_id=1, source_target_pairs={{0,16},{4,20},{8,24},{12,28},{16,0},{20,4},{24,8},{28,12},{1,17},{... | collective-permute-start | bytes 1179656 | tf_op jit(solution)/shard_map/ppermute | solution.py:877
  300.8 89.7 %collective-permute-start.65 = (f32[8,1024]{1,0:T(8,128)S(1)}, f32[8,1024]{1,0:T(8,128)S(1)}, u32[]{:S(2)}, u32[]{:S(2)}) collective-permute-start(f32[8,1024]{1,0:T(8,128)S(1)} %add.936), channel_id=1, source_target_pairs={{0,16},{4,20},{8,24},{12,28},{16,0},{20,4},{24,8},{28,12},{1,17},{... | collective-permute-start | bytes 98312 | tf_op jit(solution)/shard_map/ppermute | solution.py:877
  327.8 20.9 %collective-permute-start.13 = (bf16[2,2,2,128,256]{4,3,2,1,0:T(8,128)(2,1)S(1)}, bf16[2,2,2,128,256]{4,3,2,1,0:T(8,128)(2,1)S(1)}, u32[]{:S(2)}, u32[]{:S(2)}) collective-permute-start(bf16[2,2,2,128,256]{4,3,2,1,0:T(8,128)(2,1)S(1)} %fusion.4), channel_id=1, source_target_pairs={{0,8},{4,12},{8,0},{12,4},{16,24},{20,28},{24,16},{28,20},{1,9},{5... | collective-permute-start | bytes 1572872 | tf_op jit(solution)/shard_map/ppermute | solution.py:877
  343.6 47.7 %collective-permute-start.45 = (bf16[128,768]{1,0:T(8,128)(2,1)S(1)}, bf16[128,768]{1,0:T(8,128)(2,1)S(1)}, u32[]{:S(2)}, u32[]{:S(2)}) collective-permute-start(bf16[128,768]{1,0:T(8,128)(2,1)S(1)} %get-tuple-element.86.refs_0_), channel_id=1, source_target_pairs={{0,1},{1,0},{2,3},{3,2},{4,5},{5,4},{6,7},{7,6},{8,9},{9,8},{10,11... | collective-permute-start | bytes 589832 | tf_op jit(solution)/shard_map/ppermute | solution.py:877
  360.1 32.5 %collective-permute-start.46 = (bf16[128,768]{1,0:T(8,128)(2,1)S(1)}, bf16[128,768]{1,0:T(8,128)(2,1)S(1)}, u32[]{:S(2)}, u32[]{:S(2)}) collective-permute-start(bf16[128,768]{1,0:T(8,128)(2,1)S(1)} %get-tuple-element.86.refs_0_), channel_id=1, source_target_pairs={{0,2},{1,3},{2,0},{3,1},{4,6},{5,7},{6,4},{7,5},{8,10},{9,11},{10,... | collective-permute-start | bytes 589832 | tf_op jit(solution)/shard_map/ppermute | solution.py:877
  369.0 24.1 %collective-permute-start.48 = (bf16[128,768]{1,0:T(8,128)(2,1)S(1)}, bf16[128,768]{1,0:T(8,128)(2,1)S(1)}, u32[]{:S(2)}, u32[]{:S(2)}) collective-permute-start(bf16[128,768]{1,0:T(8,128)(2,1)S(1)} %get-tuple-element.85), channel_id=1, source_target_pairs={{0,4},{4,0},{8,12},{12,8},{16,20},{20,16},{24,28},{28,24},{1,5},{5... | collective-permute-start | bytes 589832 | tf_op jit(solution)/shard_map/ppermute | solution.py:877
  (77 other events, 989.4 us)
